TPU v7x, 32 devices: a whole 2x2x4 slice. The times are simulated.
32 devices in a mesh: slab: 8 (over y, x, core), group: 4 (over z).
Axes of the slice: x: 2, y: 2, z: 4, core: 2. Of those that a mesh axis runs over, the one named last changes fastest.
Arguments:
- grads: bfloat16 [8, 2048, 512], P('group', 'slab'), may hold values from -64 to 64
- grad_slot: int32 [4, 2], P('group'), may hold values from 0 to 1, each once within a row
- momentum: bfloat16 [8, 2048, 512], P('group', 'slab'), may hold values from -6 to 6
Outputs:
- new_momentum: bfloat16 [8, 2048, 512], P('group', 'slab')
- update: bfloat16 [8, 2048, 512], P('group', 'slab')
All inputs are finite; a program needn't handle non-finite values.
Results may differ from a plain program's by a relative error of at most 0.0071.
Values may be sent and summed in bfloat16 or wider, within the bound.
No kernel may reach another device: no remote copies, remote signals or barrier semaphores. Data moves between devices by JAX's collectives and lax.ppermute only.
A program may use at most 64 MiB of HBM per device.

v0:
```python
import jax
import jax.numpy as jnp
from jax import lax
from jax.sharding import PartitionSpec as P

M = 2048
SHARE = 4
ITERS = 2


COEF_A = 3.4445
COEF_B = -4.775
COEF_C = 2.0315
DECAY_RATE = 0.95


def form_gram(matrix):
    return lax.dot_general(
        matrix, matrix, (((0,), (0,)), ((), ())), preferred_element_type=jnp.float32
    )


def newton_factor(current):
    identity = jnp.eye(current.shape[0], dtype=jnp.float32)
    product = current
    for iteration in range(ITERS):
        rounded = current.astype(jnp.bfloat16)
        squared = jnp.dot(rounded, rounded, preferred_element_type=jnp.float32)
        poly = COEF_A * identity + COEF_B * current + COEF_C * squared
        poly_half = poly.astype(jnp.bfloat16)
        if iteration == 0:
            product = poly
        else:
            product = jnp.dot(
                product.astype(jnp.bfloat16), poly_half, preferred_element_type=jnp.float32
            )
        if iteration < ITERS - 1:
            halfway = jnp.dot(rounded, poly_half, preferred_element_type=jnp.float32).astype(
                jnp.bfloat16
            )
            current = jnp.dot(poly_half, halfway, preferred_element_type=jnp.float32)
    return product


def on_device(grads, grad_slot, momentum):
    partial_sq = jnp.sum(jnp.square(grads.astype(jnp.float32)))
    total_sq = lax.psum(partial_sq, ("slab", "group"))
    entries = grads.size * lax.axis_size("slab") * lax.axis_size("group")
    root_mean = jnp.sqrt(total_sq / entries + 1e-06)
    clip_factor = jnp.minimum(1.0, 1.0 / root_mean)
    ordered = jnp.take(grads, grad_slot[0], axis=0)
    new_momentum = (
        DECAY_RATE * momentum.astype(jnp.float32) + clip_factor * ordered.astype(jnp.float32)
    ).astype(jnp.bfloat16)
    experts, slab_rows, columns = new_momentum.shape
    slab_count = lax.axis_size("slab")
    quarter = slab_rows // SHARE
    outgoing = jnp.repeat(new_momentum, SHARE, axis=0)
    whole_matrix = lax.all_to_all(outgoing, "slab", split_axis=0, concat_axis=1, tiled=True)[0]
    gram_matrix = form_gram(whole_matrix)
    offset = lax.axis_index("slab") % SHARE * quarter
    own_rows = lax.dynamic_slice_in_dim(
        whole_matrix.reshape(slab_count, slab_rows, columns), offset, quarter, 1
    )
    frobenius = jnp.trace(gram_matrix) + 1e-06
    product = newton_factor(gram_matrix / frobenius)
    scaled_q = (product / jnp.sqrt(frobenius)).astype(jnp.bfloat16)
    result_rows = jnp.dot(
        own_rows.reshape(slab_count * quarter, columns),
        scaled_q,
        preferred_element_type=jnp.float32,
    )
    scaled_rows = (
        (jnp.sqrt(jnp.float32(M)) * result_rows)
        .astype(jnp.bfloat16)
        .reshape(slab_count, quarter, columns)
    )
    returned = lax.all_to_all(scaled_rows, "slab", split_axis=0, concat_axis=0, tiled=True)
    update = returned.reshape(experts, SHARE, quarter, columns).reshape(experts, slab_rows, columns)
    return (new_momentum, update)


def solution(mesh):
    in_specs = (P("group", "slab", None), P("group", None), P("group", "slab", None))
    out_specs = (P("group", "slab", None), P("group", "slab", None))
    return jax.shard_map(
        on_device, mesh=mesh, in_specs=in_specs, out_specs=out_specs, check_vma=False
    )
```

profile of v0, /device:TPU:0, one launch (start us, length us, event | category | flops | bytes accessed | tf_op | source)
XLA Modules:
  0.0 104.4 jit_solution(8624647279168940296)
XLA Ops:
  0.6 0.7 fusion.13
  1.3 0.7 compare_and_fusion
  2.0 1.9 %multiply_reduce_fusion = f32[]{:T(128)} fusion(bf16[2,256,512]{2,1,0:T(8,128)(2,1)} %param.3), kind=kLoop, calls=%fused_computation.19 | loop fusion | flops 786431 | bytes 524292 | tf_op jit(solution)/shard_map/reduce_sum | solution.py:46
  3.9 1.6 %gather_fusion = bf16[2,256,512]{2,1,0:T(8,128)(2,1)S(1)} fusion(bf16[2,256,512]{2,1,0:T(8,128)(2,1)} %param.3, s32[1024]{0:T(1024)S(1)} %pad_clamp_fusion), kind=kCustom, calls=%fused_computation | custom fusion | bytes 1048584 | tf_op jit(solution)/shard_map/jit(_take)/gather | solution.py:51
  5.5 42.3 %psum.7 = f32[]{:T(128)} all-reduce(f32[]{:T(128)} %multiply_reduce_fusion), channel_id=1, replica_groups=mesh['slab'=8,'group'=4] {'slab','group'}, use_global_device_ids=true, to_apply=%region_1.0 | all-reduce | flops 1 | bytes 8 | tf_op jit(solution)/shard_map/psum | solution.py:47
  48.5 1.3 %add_convert_fusion = bf16[2,256,512]{2,1,0:T(8,128)(2,1)S(1)} fusion(bf16[2,256,512]{2,1,0:T(8,128)(2,1)} %param.5, bf16[2,256,512]{2,1,0:T(8,128)(2,1)S(1)} %gather_fusion, f32[]{:T(128)S(6)} %min.3, pred[2]{0:T(512)(128)(4,1)S(1)} %compare_and_fusion), kind=kLoop, calls=%fused_computation.18 | loop fusion | flops 1835008 | bytes 1572870 | tf_op jit(solution)/shard_map/convert_element_type | solution.py:54
  49.8 0.0 copy-start
  49.8 1.5 %broadcast_in_dim.17 = bf16[2,4,256,512]{3,2,1,0:T(8,128)(2,1)} broadcast(bf16[2,256,512]{2,1,0:T(8,128)(2,1)S(1)} %add_convert_fusion), dimensions={0,2,3} | broadcast | bytes 2621440 | tf_op jit(solution)/shard_map/broadcast_in_dim | solution.py:58
  51.3 0.0 copy-done
  51.3 3.7 %all-to-all-start = ((bf16[8,256,512]{2,1,0:T(8,128)(2,1)}), bf16[8,256,512]{2,1,0:T(8,128)(2,1)S(1)}, u32[]{:S(2)}, u32[]{:S(2)}) async-start(bf16[8,256,512]{2,1,0:T(8,128)(2,1)} %bitcast.3), calls=%async_computation | async-start | bytes 4194304 | tf_op jit(solution)/shard_map/all_to_all | solution.py:59
  55.1 26.6 %all-to-all-done = bf16[8,256,512]{2,1,0:T(8,128)(2,1)S(1)} async-done(((bf16[8,256,512]{2,1,0:T(8,128)(2,1)}), bf16[8,256,512]{2,1,0:T(8,128)(2,1)S(1)}, u32[]{:S(2)}, u32[]{:S(2)}) %all-to-all-start) | async-done | bytes 2097184 | tf_op jit(solution)/shard_map/all_to_all | solution.py:59
  81.7 1.9 %select_reduce_fusion = (f32[]{:T(128)}, f32[512,512]{1,0:T(8,128)S(1)}) fusion(bf16[8,256,512]{2,1,0:T(8,128)(2,1)S(1)} %all-to-all-done), kind=kOutput, calls=%fused_computation.16 | convolution fusion | flops 1074528256 | bytes 3145732 | tf_op jit(solution)/shard_map/dot_general | solution.py:18
  83.6 0.0 copy-start.1
  84.3 0.3 copy-done.1
  84.6 1.3 %fusion.2 = bf16[512,512]{1,0:T(8,128)(2,1)} fusion(f32[512,512]{1,0:T(8,128)S(1)} %get-tuple-element.3, f32[]{:T(128)S(6)} %add.51), kind=kOutput, calls=%fused_computation.10 | convolution fusion | flops 271056896 | bytes 1572868 | tf_op jit(solution)/shard_map/dot_general | solution.py:28
  85.9 2.3 %fusion.6 = f32[512,512]{1,0:T(8,128)S(1)} fusion(bf16[512,512]{1,0:T(8,128)(2,1)} %fusion.2, f32[512,512]{1,0:T(8,128)} %copy-done.1, f32[]{:T(128)S(6)} %add.51), kind=kOutput, calls=%fused_computation.15 | convolution fusion | flops 537657344 | bytes 2621444 | tf_op jit(solution)/shard_map/dot_general | solution.py:41
  88.2 1.3 %fusion.3 = bf16[512,512]{1,0:T(8,128)(2,1)} fusion(f32[512,512]{1,0:T(8,128)S(1)} %fusion.6), kind=kOutput, calls=%fused_computation.11 | convolution fusion | flops 270532608 | bytes 1572864 | tf_op jit(solution)/shard_map/dot_general | solution.py:28
  89.5 2.0 %fusion.5 = bf16[512,512]{1,0:T(8,128)(2,1)S(1)} fusion(bf16[512,512]{1,0:T(8,128)(2,1)S(1)} %bitcast.21, bf16[512,512]{1,0:T(8,128)(2,1)} %fusion.2, bf16[512,512]{1,0:T(8,128)(2,1)} %fusion.3, f32[]{:T(128)S(6)} %sqrt.7), kind=kOutput, calls=%fused_computation.14 | convolution fusion | flops 537919488 | bytes 2097156 | tf_op jit(solution)/shard_map/dot_general | solution.py:68
  91.5 12.2 %all_to_all.14 = bf16[8,64,512]{2,1,0:T(8,128)(2,1)S(1)} all-to-all(bf16[8,64,512]{2,1,0:T(8,128)(2,1)S(1)} %bitcast.20), channel_id=1, replica_groups=mesh['slab'=8,'group'=4] {'slab'}, dimensions={0} | all-to-all | bytes 1048576 | tf_op jit(solution)/shard_map/all_to_all | solution.py:78
  103.6 0.8 copy.9
  (2 shorter events, 0.0 us)
Async XLA Ops:
  49.8 1.5 %copy-start = (bf16[2,256,512]{2,1,0:T(8,128)(2,1)}, bf16[2,256,512]{2,1,0:T(8,128)(2,1)S(1)}, u32[]{:S(2)}) copy-start(bf16[2,256,512]{2,1,0:T(8,128)(2,1)S(1)} %add_convert_fusion) | copy-start | bytes 1572868
  51.3 30.4 %all-to-all-start = ((bf16[8,256,512]{2,1,0:T(8,128)(2,1)}), bf16[8,256,512]{2,1,0:T(8,128)(2,1)S(1)}, u32[]{:S(2)}, u32[]{:S(2)}) async-start(bf16[8,256,512]{2,1,0:T(8,128)(2,1)} %bitcast.3), calls=%async_computation | async-start | bytes 4194304 | tf_op jit(solution)/shard_map/all_to_all | solution.py:59
  83.6 1.0 copy-start.1
where the time goes:
time: 105 us; the launch traced here: 104 us
  blocking collectives  54.4 us (52%)
  waiting for transfers between devices  26.6 us (25%)
  matrix products  8.69 us (8%)
  other arithmetic  4.56 us (4%)
  local copies, waits for them, and re-layouts  4.28 us (4%)
  starting transfers between devices  3.74 us (4%)
  between operations  2.06 us (2%)
    psum x1, blocking collectives, on_device(): total_sq = lax.psum(partial_sq, ('slab', 'group'))  42.3 us
    all_to_all x1, waiting for transfers between devices, on_device(): lax.all_to_all(outgoing, 'slab', split_axis=0, concat_axis=1, tiled=True)[0]  26.6 us
    all_to_all x1, blocking collectives, on_device(): lax.all_to_all(scaled_rows, 'slab', split_axis=0, concat_axis=0, tiled=True)  12.2 us
    all_to_all x1, starting transfers between devices, on_device(): lax.all_to_all(outgoing, 'slab', split_axis=0, concat_axis=1, tiled=True)[0]  3.74 us
    dot_general x2, matrix products, newton_factor(): squared = jnp.dot(rounded, rounded, preferred_element_type=jnp.float32)  2.54 us
    dot_general x1, matrix products, newton_factor(): current = jnp.dot(poly_half, halfway, preferred_element_type=jnp.float32)  2.3 us
  transfers between devices with their start and end apart: 1, of which 1 were waited for; matrix products, arithmetic and copies ran while one was open for 0% of the time, Pallas kernels for 0%

commit v1 on v0

v1 whole, which is shorter than its diff:
```python
import functools

import jax
import jax.numpy as jnp
from jax import lax
from jax.experimental import pallas as pl
from jax.experimental.pallas import tpu as pltpu
from jax.sharding import PartitionSpec as P

M = 2048
ITERS = 2

COEF_A = 3.4445
COEF_B = -4.775
COEF_C = 2.0315
DECAY_RATE = 0.95

AXES = ("slab", "group")
VMEM_LIMIT = 24 * 1024 * 1024
HALVES = (
    (((1, 0), (2, 0), (2, 1)), (0, 1)),
    (((3, 0), (3, 1), (3, 2)), (2, 3)),
)
BLOCKS = 4
TAIL = 16


def params(semantics=None):
    return pltpu.CompilerParams(vmem_limit_bytes=VMEM_LIMIT, dimension_semantics=semantics)


def cost(flops, bytes_accessed):
    return pl.CostEstimate(flops=flops, bytes_accessed=bytes_accessed, transcendentals=0)


def squares_kernel(grads_ref, out_ref):
    values = grads_ref[...].astype(jnp.float32)
    experts, rows, columns = values.shape
    total = jnp.sum((values * values).reshape(experts * rows, columns), axis=0, keepdims=True)
    lanes = sum(total[:, at : at + 128] for at in range(0, columns, 128))
    out_ref[...] = jnp.broadcast_to(lanes, out_ref.shape)


def sum_squares(grads, copies):
    return pl.pallas_call(
        squares_kernel,
        out_shape=jax.ShapeDtypeStruct((copies, 128), jnp.float32),
        in_specs=[pl.BlockSpec(memory_space=pltpu.VMEM)],
        out_specs=pl.BlockSpec(memory_space=pltpu.VMEM),
        compiler_params=params(),
        cost_estimate=cost(2 * grads.size, 2 * grads.size),
        name="sum_squares",
    )(grads)


def fresh_momentum(momentum, gradient, clip):
    return (
        DECAY_RATE * momentum.astype(jnp.float32) + clip * gradient.astype(jnp.float32)
    ).astype(jnp.bfloat16)


def grid_index(shape):
    return (
        lax.broadcasted_iota(jnp.int32, shape, 0),
        lax.broadcasted_iota(jnp.int32, shape, 1),
    )


def gram_kernel(
    entries, place_ref, squares_ref, m0_ref, g0_ref, m1_ref, g1_ref, pa_ref, pb_ref, clip_ref, rows_ref, gram_ref
):
    total = jnp.sum(squares_ref[...], keepdims=True)
    root_mean = jnp.sqrt(total / entries + 1e-06)
    clip = jnp.minimum(1.0, 1.0 / root_mean)
    clip_ref[...] = jnp.broadcast_to(clip, clip_ref.shape)
    rows = m0_ref.shape[1]
    rows_ref[:rows, :] = fresh_momentum(m0_ref[0], g0_ref[0], clip)
    rows_ref[rows:, :] = fresh_momentum(m1_ref[0], g1_ref[0], clip)
    fresh = rows_ref[...]
    gram_ref[...] = lax.dot_general(
        fresh, fresh, (((0,), (0,)), ((), ())), preferred_element_type=jnp.float32
    )
    size = gram_ref.shape[0] // BLOCKS
    row, column = grid_index((size, size))

    def block(i, j):
        return gram_ref[i * size : (i + 1) * size, j * size : (j + 1) * size]

    for (lower, (first, second)), out_ref in zip(HALVES, (pa_ref, pb_ref)):
        for at, (i, j) in enumerate(lower):
            out_ref[0, at * size : (at + 1) * size, :] = block(i, j).astype(jnp.bfloat16)
        last = block(second, second)
        shared = jnp.where(column <= row, block(first, first), last)
        out_ref[0, 3 * size : 4 * size, :] = shared.astype(jnp.bfloat16)
        diagonal = jnp.sum(jnp.where(column == row, last, 0.0), axis=0, keepdims=True)
        out_ref[0, 4 * size :, :] = jnp.broadcast_to(diagonal, (TAIL, size)).astype(jnp.bfloat16)


def packed_grams(place, squares, momentum, grads, other_momentum, other_grads, entries):
    experts, rows, columns = momentum.shape
    half = experts // 2
    size = columns // BLOCKS
    packed = jax.ShapeDtypeStruct((half, 4 * size + TAIL, size), jnp.bfloat16)
    packed_spec = pl.BlockSpec((1, 4 * size + TAIL, size), lambda i, place: (i, 0, 0))
    by_expert = pl.BlockSpec((1, rows, columns), lambda i, place: (place[0] * half + i, 0, 0))
    by_slot = pl.BlockSpec(
        (1, rows, columns), lambda i, place: (place[1 + place[0] * half + i], 0, 0)
    )
    return pl.pallas_call(
        functools.partial(gram_kernel, entries),
        grid_spec=pltpu.PrefetchScalarGridSpec(
            num_scalar_prefetch=1,
            grid=(half,),
            in_specs=[
                pl.BlockSpec(squares.shape, lambda i, place: (0, 0)),
                by_expert,
                by_slot,
                by_expert,
                by_slot,
            ],
            out_specs=[
                packed_spec,
                packed_spec,
                pl.BlockSpec((8, 128), lambda i, place: (0, 0)),
            ],
            scratch_shapes=[
                pltpu.VMEM((2 * rows, columns), jnp.bfloat16),
                pltpu.VMEM((columns, columns), jnp.float32),
            ],
        ),
        out_shape=[packed, packed, jax.ShapeDtypeStruct((8, 128), jnp.float32)],
        compiler_params=params(("arbitrary",)),
        cost_estimate=cost(
            4 * half * rows * columns * columns, 2 * (4 * half * rows * columns + 2 * packed.size)
        ),
        name="packed_grams",
    )(place, squares, momentum, grads, other_momentum, other_grads)


def momentum_kernel(place_ref, clip_ref, momentum_ref, grads_ref, out_ref):
    out_ref[0] = fresh_momentum(momentum_ref[0], grads_ref[0], clip_ref[:1, :1])


def update_momentum(place, clip, momentum, grads):
    experts, rows, columns = momentum.shape
    by_expert = pl.BlockSpec((1, rows, columns), lambda i, place: (i, 0, 0))
    return pl.pallas_call(
        momentum_kernel,
        grid_spec=pltpu.PrefetchScalarGridSpec(
            num_scalar_prefetch=1,
            grid=(experts,),
            in_specs=[
                pl.BlockSpec(clip.shape, lambda i, place: (0, 0)),
                by_expert,
                pl.BlockSpec((1, rows, columns), lambda i, place: (place[1 + i], 0, 0)),
            ],
            out_specs=by_expert,
        ),
        out_shape=jax.ShapeDtypeStruct(momentum.shape, jnp.bfloat16),
        compiler_params=params(("arbitrary",)),
        cost_estimate=cost(3 * momentum.size, 6 * momentum.size),
        name="update_momentum",
    )(place, clip, momentum, grads)


def bf16_dot(left, right):
    return jnp.dot(left, right, preferred_element_type=jnp.float32)


def newton_kernel(a0_ref, a1_ref, b0_ref, b1_ref, out_ref, frob_ref, gram_ref):
    columns = gram_ref.shape[0]
    size = columns // BLOCKS
    row, column = grid_index((size, size))
    for (lower, (first, second)), (x_ref, y_ref) in zip(
        HALVES, ((a0_ref, a1_ref), (b0_ref, b1_ref))
    ):

        def piece(at, end):
            return x_ref[0, at:end, :].astype(jnp.float32) + y_ref[0, at:end, :].astype(
                jnp.float32
            )

        def put(i, j, value):
            gram_ref[i * size : (i + 1) * size, j * size : (j + 1) * size] = value

        for at, (i, j) in enumerate(lower):
            value = piece(at * size, (at + 1) * size)
            put(i, j, value)
            put(j, i, value.T)
        shared = piece(3 * size, 4 * size)
        flipped = shared.T
        diagonal = piece(4 * size, 4 * size + TAIL)[:1, :]
        put(first, first, jnp.where(column <= row, shared, flipped))
        put(
            second,
            second,
            jnp.where(
                column == row, diagonal, jnp.where(column > row, shared, flipped)
            ),
        )
    row, column = grid_index((columns, columns))
    on_diagonal = row == column
    gram = gram_ref[...]
    frob = jnp.sum(jnp.where(on_diagonal, gram, 0.0), keepdims=True) + 1e-06
    current = gram / frob
    product = None
    for iteration in range(ITERS):
        rounded = current.astype(jnp.bfloat16)
        squared = bf16_dot(rounded, rounded)
        poly = (
            jnp.where(on_diagonal, COEF_A, 0.0) + COEF_B * current + COEF_C * squared
        )
        poly_half = poly.astype(jnp.bfloat16)
        if iteration == 0:
            product = poly
        else:
            product = bf16_dot(product.astype(jnp.bfloat16), poly_half)
        if iteration < ITERS - 1:
            halfway = bf16_dot(rounded, poly_half).astype(jnp.bfloat16)
            current = bf16_dot(poly_half, halfway)
    out_ref[0] = (product / jnp.sqrt(frob)).astype(jnp.bfloat16)


def newton_factors(a0, a1, b0, b1, columns):
    half, depth, size = a0.shape
    packed = pl.BlockSpec((1, depth, size), lambda i: (i, 0, 0))
    return pl.pallas_call(
        newton_kernel,
        grid=(half,),
        in_specs=[packed] * 4,
        out_specs=pl.BlockSpec((1, columns, columns), lambda i: (i, 0, 0)),
        out_shape=jax.ShapeDtypeStruct((half, columns, columns), jnp.bfloat16),
        scratch_shapes=[
            pltpu.VMEM((8, 128), jnp.float32),
            pltpu.VMEM((columns, columns), jnp.float32),
        ],
        compiler_params=params(("arbitrary",)),
        cost_estimate=cost(
            10 * half * columns**3, 2 * (4 * a0.size + half * columns * columns)
        ),
        name="newton_factors",
    )(a0, a1, b0, b1)


def apply_kernel(place_ref, rows_ref, factor_ref, *refs):
    out_ref = refs[-1]
    result = bf16_dot(rows_ref[0], factor_ref[0])
    out_ref[0] = (jnp.sqrt(jnp.float32(M)) * result).astype(jnp.bfloat16)


def apply_factors(place, fresh, factors, update=None):
    experts, rows, columns = fresh.shape
    half = experts // 2
    other = update is not None

    def at_expert(i, place):
        core = 1 - place[0] if other else place[0]
        return (core * half + i, 0, 0)

    return pl.pallas_call(
        apply_kernel,
        grid_spec=pltpu.PrefetchScalarGridSpec(
            num_scalar_prefetch=1,
            grid=(half,),
            in_specs=[
                pl.BlockSpec((1, rows, columns), at_expert),
                pl.BlockSpec((1, columns, columns), lambda i, place: (i, 0, 0)),
            ]
            + ([pl.BlockSpec(memory_space=pl.ANY)] if other else []),
            out_specs=pl.BlockSpec((1, rows, columns), at_expert),
        ),
        out_shape=jax.ShapeDtypeStruct(fresh.shape, jnp.bfloat16),
        input_output_aliases={3: 0} if other else {},
        compiler_params=params(("arbitrary",)),
        cost_estimate=cost(
            2 * half * rows * columns * columns,
            2 * half * (2 * rows * columns + columns * columns),
        ),
        name="apply_other" if other else "apply_own",
    )(*((place, fresh, factors) + ((update,) if other else ())))


def on_device(grads, grad_slot, momentum):
    slab_count = lax.axis_size("slab")
    devices = slab_count * lax.axis_size("group")
    core = lax.axis_index("slab") % 2
    place = jnp.concatenate([core[None].astype(jnp.int32), grad_slot[0].astype(jnp.int32)])

    def swap(value, bit):
        return lax.ppermute(value, "slab", [(i, i ^ bit) for i in range(slab_count)])

    other_grads, other_momentum = swap(grads, 1), swap(momentum, 1)
    squares = lax.all_to_all(sum_squares(grads, devices), AXES, 0, 0, tiled=True)
    a, b, clip = packed_grams(
        place, squares, momentum, grads, other_momentum, other_grads, grads.size * devices
    )
    bits = []
    while 2 << len(bits) < slab_count:
        bits.append(2 << len(bits))
    turned = bits[len(bits) // 2 :] + bits[: len(bits) // 2]
    for step, (bit_a, bit_b) in enumerate(zip(bits, turned)):
        a1, b1 = swap(a, bit_a), swap(b, bit_b)
        if step < len(bits) - 1:
            a = (a.astype(jnp.float32) + a1.astype(jnp.float32)).astype(jnp.bfloat16)
            b = (b.astype(jnp.float32) + b1.astype(jnp.float32)).astype(jnp.bfloat16)
    fresh = update_momentum(place, clip, momentum, grads)
    factors = newton_factors(a, a1, b, b1, grads.shape[2])
    other_factors = swap(factors, 1)
    update = apply_factors(place, fresh, factors)
    update = apply_factors(place, fresh, other_factors, update)
    return (fresh, update)


def solution(mesh):
    in_specs = (P("group", "slab", None), P("group", None), P("group", "slab", None))
    out_specs = (P("group", "slab", None), P("group", "slab", None))
    return jax.shard_map(
        on_device, mesh=mesh, in_specs=in_specs, out_specs=out_specs, check_vma=False
    )
```

time: 105 us -> 38.9 us (0.37)
  blocking collectives: 54.4 us -> 0 us
  waiting for transfers between devices: 26.6 us -> 14.4 us
  matrix products: 8.69 us -> 0 us
  Pallas kernels: 0 us -> 8.59 us
  starting transfers between devices: 3.74 us -> 10.9 us
  other arithmetic: 4.56 us -> 0.15 us
  between operations: 2.06 us -> 0.72 us
    psum x1 -> x0, blocking collectives: 42.3 us -> none  [on_device(): total_sq = lax.psum(partial_sq, ('slab', 'group'))]
    all_to_all x1, waiting for transfers between devices: 26.6 us -> 6.35 us  [on_device(): lax.all_to_all(sum_squares(grads, devices), AXES, 0, 0, tiled=True)]
    all_to_all x1 -> x0, blocking collectives: 12.2 us -> none  [on_device(): lax.all_to_all(scaled_rows, 'slab', split_axis=0, concat_axis=0, tiled=True)]
    dot_general x5 -> x0, matrix products: 8.69 us -> none  [the longest x2 2.54 us: newton_factor(): squared = jnp.dot(rounded, rounded, preferred_element_type=jnp.float32)]
    pallas_call x0 -> x6, Pallas kernels: none -> 8.59 us  [the longest x2 3.09 us: apply_factors(): pl.pallas_call(apply_kernel, grid_spec=pltpu.PrefetchScalarGridSpec(num_s...]
    ppermute x0 -> x7, waiting for transfers between devices: none -> 8.08 us  [swap(): lax.ppermute(value, 'slab', [(i, i ^ bit) for i in range(slab_count)])]
    ppermute x0 -> x7, starting transfers between devices: none -> 3.65 us  [swap(): lax.ppermute(value, 'slab', [(i, i ^ bit) for i in range(slab_count)])]
    all_to_all x1, starting transfers between devices: 3.74 us -> 7.27 us  [on_device(): lax.all_to_all(sum_squares(grads, devices), AXES, 0, 0, tiled=True)]
  transfers between devices with their start and end apart: 1 -> 8, of which waited for: 1 -> 4; matrix products, arithmetic and copies ran while one was open for 0% -> 0% of each run, Pallas kernels for 0% -> 10%
where the time goes in v1:
time: 38.9 us; the launch traced here: 38.6 us
  waiting for transfers between devices  14.4 us (37%)
  starting transfers between devices  10.9 us (28%)
  Pallas kernels  8.59 us (22%)
  local copies, waits for them, and re-layouts  3.78 us (10%)
  between operations  0.72 us (2%)
    ppermute x7, waiting for transfers between devices, swap(): lax.ppermute(value, 'slab', [(i, i ^ bit) for i in range(slab_count)])  8.08 us
    all_to_all x1, starting transfers between devices, on_device(): lax.all_to_all(sum_squares(grads, devices), AXES, 0, 0, tiled=True)  7.27 us
    all_to_all x1, waiting for transfers between devices, on_device(): lax.all_to_all(sum_squares(grads, devices), AXES, 0, 0, tiled=True)  6.35 us
    unnamed x12, local copies, waits for them, and re-layouts  3.78 us
    ppermute x7, starting transfers between devices, swap(): lax.ppermute(value, 'slab', [(i, i ^ bit) for i in range(slab_count)])  3.65 us
    pallas_call x2, Pallas kernels, apply_factors(): pl.pallas_call(apply_kernel, grid_spec=pltpu.PrefetchScalarGridSpec(num_s...  3.09 us
    pallas_call x1, Pallas kernels, newton_factors(): pl.pallas_call(newton_kernel, grid=(half,), in_specs=[packed] * 4, out_sp...  2.05 us
    pallas_call x1, Pallas kernels, update_momentum(): pl.pallas_call(momentum_kernel, grid_spec=pltpu.PrefetchScalarGridSpec(nu...  1.61 us
  transfers between devices with their start and end apart: 8, of which 4 were waited for; matrix products, arithmetic and copies ran while one was open for 0% of the time, Pallas kernels for 10%

profile of v1, /device:TPU:0, one launch (start us, length us, event | category | flops | bytes accessed | tf_op | source)
XLA Modules:
  0.0 38.6 jit_solution(13540831573599025137)
XLA Ops:
  0.6 0.5 %collective-permute-start = (bf16[2,256,512]{2,1,0:T(8,128)(2,1)}, bf16[2,256,512]{2,1,0:T(8,128)(2,1)S(1)}, u32[]{:S(2)}, u32[]{:S(2)}) collective-permute-start(bf16[2,256,512]{2,1,0:T(8,128)(2,1)} %momentum_ref.1), channel_id=1, source_target_pairs={{0,4},{4,0},{8,12},{12,8},{16,20},{20,16},{24,28},{28,24},{1,5},{5... | collective-permute-start | bytes 1572872 | tf_op jit(solution)/shard_map/ppermute | solution.py:290
  1.1 0.1 collective-permute-start.1
  1.2 0.0 copy-start
  1.2 1.0 %copy-done = bf16[2,256,512]{2,1,0:T(8,128)(2,1)S(1)} copy-done((bf16[2,256,512]{2,1,0:T(8,128)(2,1)S(1)}, bf16[2,256,512]{2,1,0:T(8,128)(2,1)}, u32[]{:S(2)}) %copy-start) | copy-done | bytes 524312
  2.3 0.0 copy-start.1
  2.3 0.7 %sum_squares.1 = f32[32,128]{1,0:T(8,128)} custom-call(bf16[2,256,512]{2,1,0:T(8,128)(2,1)S(1)} %copy-done), custom_call_target="tpu_custom_call" | custom-call | flops 524288 | bytes 524288 | tf_op jit(solution)/shard_map/sum_squares/pallas_call | solution.py:45
  2.9 7.3 %all-to-all-start = ((f32[32,1,128]{2,1,0:T(1,128)}), f32[32,1,128]{2,1,0:T(1,128)S(1)}, u32[]{:S(2)}, u32[]{:S(2)}) async-start(f32[32,1,128]{2,1,0:T(1,128)} %bitcast.3), calls=%async_computation | async-start | bytes 32768 | tf_op jit(solution)/shard_map/all_to_all | solution.py:293
  10.2 0.0 copy-start.5
  10.2 0.6 %copy-done.5 = s32[1,2]{1,0:T(1,128)S(1)} copy-done((s32[1,2]{1,0:T(1,128)S(1)}, s32[1,2]{1,0:T(1,128)}, u32[]{:S(2)}) %copy-start.5) | copy-done | bytes 32
  10.9 0.1 pad_add_fusion.place_ref
  11.0 6.4 %all-to-all-done = f32[32,1,128]{2,1,0:T(1,128)S(1)} async-done(((f32[32,1,128]{2,1,0:T(1,128)}), f32[32,1,128]{2,1,0:T(1,128)S(1)}, u32[]{:S(2)}, u32[]{:S(2)}) %all-to-all-start) | async-done | bytes 16416 | tf_op jit(solution)/shard_map/all_to_all | solution.py:293
  17.3 0.0 collective-permute-done.m1_ref
  17.3 0.0 collective-permute-done.1.g1_ref
  17.3 0.0 copy-done.1
  17.3 0.0 copy-start.3
  17.3 1.0 %copy-done.3 = bf16[2,256,512]{2,1,0:T(8,128)(2,1)S(1)} copy-done((bf16[2,256,512]{2,1,0:T(8,128)(2,1)S(1)}, bf16[2,256,512]{2,1,0:T(8,128)(2,1)}, u32[]{:S(2)}) %copy-start.3) | copy-done | bytes 524312
  18.4 1.2 %packed_grams.1 = (bf16[1,528,128]{2,1,0:T(8,128)(2,1)S(1)}, bf16[1,528,128]{2,1,0:T(8,128)(2,1)S(1)}, f32[8,128]{1,0:T(8,128)S(1)}) custom-call(s32[3]{0:T(128)S(1)} %pad_add_fusion.place_ref, f32[32,128]{1,0:T(8,128)S(1)} %bitcast.6, bf16[2,256,512]{2,1,0:T(8,128)(2,1)S(1)} %copy-done.3, bf16[2,256,512]{2,1,0:T(8,128)(2,1)S(1)} %copy-done.1, ...), custom_call_target="tpu_custom_call" | custom-call | flops 268435456 | bytes 1318912 | tf_op jit(solution)/shard_map/packed_grams/pallas_call | solution.py:109
  19.5 0.6 %collective-permute-start.2 = (bf16[1,528,128]{2,1,0:T(8,128)(2,1)S(1)}, bf16[1,528,128]{2,1,0:T(8,128)(2,1)S(1)}, u32[]{:S(2)}, u32[]{:S(2)}) collective-permute-start(bf16[1,528,128]{2,1,0:T(8,128)(2,1)S(1)} %get-tuple-element.6), channel_id=1, source_target_pairs={{0,8},{4,12},{8,0},{12,4},{16,24},{20,28},{24,16},{28,20},{1,9},{5... | collective-permute-start | bytes 405512 | tf_op jit(solution)/shard_map/ppermute | solution.py:290
  20.2 0.5 %collective-permute-start.4 = (bf16[1,528,128]{2,1,0:T(8,128)(2,1)S(1)}, bf16[1,528,128]{2,1,0:T(8,128)(2,1)S(1)}, u32[]{:S(2)}, u32[]{:S(2)}) collective-permute-start(bf16[1,528,128]{2,1,0:T(8,128)(2,1)S(1)} %get-tuple-element.7), channel_id=1, source_target_pairs={{0,16},{4,20},{8,24},{12,28},{16,0},{20,4},{24,8},{28,12},{1,17},{... | collective-permute-start | bytes 405512 | tf_op jit(solution)/shard_map/ppermute | solution.py:290
  20.7 4.1 %collective-permute-done.2 = bf16[1,528,128]{2,1,0:T(8,128)(2,1)S(1)} collective-permute-done((bf16[1,528,128]{2,1,0:T(8,128)(2,1)S(1)}, bf16[1,528,128]{2,1,0:T(8,128)(2,1)S(1)}, u32[]{:S(2)}, u32[]{:S(2)}) %collective-permute-start.2) | collective-permute-done | bytes 135200 | tf_op jit(solution)/shard_map/ppermute | solution.py:290
  24.9 0.7 %collective-permute-start.3 = (bf16[1,528,128]{2,1,0:T(8,128)(2,1)S(1)}, bf16[1,528,128]{2,1,0:T(8,128)(2,1)S(1)}, u32[]{:S(2)}, u32[]{:S(2)}) collective-permute-start(bf16[1,528,128]{2,1,0:T(8,128)(2,1)S(1)} %add_convert_fusion.1.a0_ref), channel_id=1, source_target_pairs={{0,16},{4,20},{8,24},{12,28},{16,0},{20,4},{24,8},{28,12},{1,17},{... | collective-permute-start | bytes 405512 | tf_op jit(solution)/shard_map/ppermute | solution.py:290
  25.6 0.0 collective-permute-done.4
  25.6 0.0 copy-start.4
  25.6 1.1 %collective-permute-start.5 = (bf16[1,528,128]{2,1,0:T(8,128)(2,1)S(1)}, bf16[1,528,128]{2,1,0:T(8,128)(2,1)S(1)}, u32[]{:S(2)}, u32[]{:S(2)}) collective-permute-start(bf16[1,528,128]{2,1,0:T(8,128)(2,1)S(1)} %add_convert_fusion.b0_ref), channel_id=1, source_target_pairs={{0,8},{4,12},{8,0},{12,4},{16,24},{20,28},{24,16},{28,20},{1,9},{5... | collective-permute-start | bytes 405512 | tf_op jit(solution)/shard_map/ppermute | solution.py:290
  26.8 3.2 %collective-permute-done.3.a1_ref = bf16[1,528,128]{2,1,0:T(8,128)(2,1)S(1)} collective-permute-done((bf16[1,528,128]{2,1,0:T(8,128)(2,1)S(1)}, bf16[1,528,128]{2,1,0:T(8,128)(2,1)S(1)}, u32[]{:S(2)}, u32[]{:S(2)}) %collective-permute-start.3) | collective-permute-done | bytes 135200 | tf_op jit(solution)/shard_map/ppermute | solution.py:290
  30.0 0.7 %collective-permute-done.5.b1_ref = bf16[1,528,128]{2,1,0:T(8,128)(2,1)S(1)} collective-permute-done((bf16[1,528,128]{2,1,0:T(8,128)(2,1)S(1)}, bf16[1,528,128]{2,1,0:T(8,128)(2,1)S(1)}, u32[]{:S(2)}, u32[]{:S(2)}) %collective-permute-start.5) | collective-permute-done | bytes 135200 | tf_op jit(solution)/shard_map/ppermute | solution.py:290
  30.7 2.1 %newton_factors.1.factor_ref = bf16[1,512,512]{2,1,0:T(8,128)(2,1)S(1)} custom-call(bf16[1,528,128]{2,1,0:T(8,128)(2,1)S(1)} %add_convert_fusion.1.a0_ref, bf16[1,528,128]{2,1,0:T(8,128)(2,1)S(1)} %collective-permute-done.3.a1_ref, bf16[1,528,128]{2,1,0:T(8,128)(2,1)S(1)} %add_convert_fusion.b0_ref, bf16[1,528,128]{2,1,0:T(8,128)(2,1)S(1)} %collective-permute-done.5.b1_ref), custom_call_target="tpu_custom_call" | custom-call | flops 1342177280 | bytes 1064960 | tf_op jit(solution)/shard_map/newton_factors/pallas_call | solution.py:227
  32.8 0.1 collective-permute-start.6
  32.8 0.0 copy-done.4
  32.8 1.6 %update_momentum.1.rows_ref = bf16[2,256,512]{2,1,0:T(8,128)(2,1)} custom-call(s32[3]{0:T(128)S(1)} %pad_add_fusion.place_ref, f32[8,128]{1,0:T(8,128)S(1)} %get-tuple-element.5.clip_ref, bf16[2,256,512]{2,1,0:T(8,128)(2,1)S(1)} %copy-done.4, bf16[2,256,512]{2,1,0:T(8,128)(2,1)S(1)} %copy-done.1), custom_call_target="tpu_custom_call" | custom-call | flops 786432 | bytes 1572864 | tf_op jit(solution)/shard_map/update_momentum/pallas_call | solution.py:147
  34.5 0.0 copy-start.2
  34.5 1.0 %copy-done.2 = bf16[2,256,512]{2,1,0:T(8,128)(2,1)S(1)} copy-done((bf16[2,256,512]{2,1,0:T(8,128)(2,1)S(1)}, bf16[2,256,512]{2,1,0:T(8,128)(2,1)}, u32[]{:S(2)}) %copy-start.2) | copy-done | bytes 524312
  35.5 1.5 %apply_own.1.refs_0_ = bf16[2,256,512]{2,1,0:T(8,128)(2,1)} custom-call(s32[3]{0:T(128)S(1)} %pad_add_fusion.place_ref, bf16[2,256,512]{2,1,0:T(8,128)(2,1)S(1)} %copy-done.2, bf16[1,512,512]{2,1,0:T(8,128)(2,1)S(1)} %newton_factors.1.factor_ref), custom_call_target="tpu_custom_call" | custom-call | flops 134217728 | bytes 1048576 | tf_op jit(solution)/shard_map/apply_own/pallas_call | solution.py:260
  37.0 0.0 collective-permute-done.6.factor_ref
  37.1 1.5 %apply_other.1 = bf16[2,256,512]{2,1,0:T(8,128)(2,1)} custom-call(s32[3]{0:T(128)S(1)} %pad_add_fusion.place_ref, bf16[2,256,512]{2,1,0:T(8,128)(2,1)S(1)} %copy-done.2, bf16[1,512,512]{2,1,0:T(8,128)(2,1)S(1)} %collective-permute-done.6.factor_ref, bf16[2,256,512]{2,1,0:T(8,128)(2,1)} %apply_own.1.refs_0_), custom_call_target="tpu_custom_call", output_to_operand_aliasing={{}: (3, {})} | custom-call | flops 134217728 | bytes 1048576 | tf_op jit(solution)/shard_map/apply_other/pallas_call | solution.py:260
  (2 shorter events, 0.1 us)
Async XLA Ops:
  0.6 16.7 %collective-permute-start = (bf16[2,256,512]{2,1,0:T(8,128)(2,1)}, bf16[2,256,512]{2,1,0:T(8,128)(2,1)S(1)}, u32[]{:S(2)}, u32[]{:S(2)}) collective-permute-start(bf16[2,256,512]{2,1,0:T(8,128)(2,1)} %momentum_ref.1), channel_id=1, source_target_pairs={{0,4},{4,0},{8,12},{12,8},{16,20},{20,16},{24,28},{28,24},{1,5},{5... | collective-permute-start | bytes 1572872 | tf_op jit(solution)/shard_map/ppermute | solution.py:290
  1.1 16.2 %collective-permute-start.1 = (bf16[2,256,512]{2,1,0:T(8,128)(2,1)}, bf16[2,256,512]{2,1,0:T(8,128)(2,1)S(1)}, u32[]{:S(2)}, u32[]{:S(2)}) collective-permute-start(bf16[2,256,512]{2,1,0:T(8,128)(2,1)} %grads_ref.3), channel_id=1, source_target_pairs={{0,4},{4,0},{8,12},{12,8},{16,20},{20,16},{24,28},{28,24},{1,5},{5... | collective-permute-start | bytes 1572872 | tf_op jit(solution)/shard_map/ppermute | solution.py:290
  1.2 1.0 %copy-start = (bf16[2,256,512]{2,1,0:T(8,128)(2,1)S(1)}, bf16[2,256,512]{2,1,0:T(8,128)(2,1)}, u32[]{:S(2)}) copy-start(bf16[2,256,512]{2,1,0:T(8,128)(2,1)} %grads_ref.3) | copy-start | bytes 1572868
  2.3 15.0 %copy-start.1 = (bf16[2,256,512]{2,1,0:T(8,128)(2,1)S(1)}, bf16[2,256,512]{2,1,0:T(8,128)(2,1)}, u32[]{:S(2)}) copy-start(bf16[2,256,512]{2,1,0:T(8,128)(2,1)} %grads_ref.3) | copy-start | bytes 1572868
  2.9 14.4 %all-to-all-start = ((f32[32,1,128]{2,1,0:T(1,128)}), f32[32,1,128]{2,1,0:T(1,128)S(1)}, u32[]{:S(2)}, u32[]{:S(2)}) async-start(f32[32,1,128]{2,1,0:T(1,128)} %bitcast.3), calls=%async_computation | async-start | bytes 32768 | tf_op jit(solution)/shard_map/all_to_all | solution.py:293
  10.2 0.7 %copy-start.5 = (s32[1,2]{1,0:T(1,128)S(1)}, s32[1,2]{1,0:T(1,128)}, u32[]{:S(2)}) copy-start(s32[1,2]{1,0:T(1,128)} %param.4) | copy-start | bytes 28
  17.3 1.0 %copy-start.3 = (bf16[2,256,512]{2,1,0:T(8,128)(2,1)S(1)}, bf16[2,256,512]{2,1,0:T(8,128)(2,1)}, u32[]{:S(2)}) copy-start(bf16[2,256,512]{2,1,0:T(8,128)(2,1)} %momentum_ref.1) | copy-start | bytes 1572868
  19.5 5.3 %collective-permute-start.2 = (bf16[1,528,128]{2,1,0:T(8,128)(2,1)S(1)}, bf16[1,528,128]{2,1,0:T(8,128)(2,1)S(1)}, u32[]{:S(2)}, u32[]{:S(2)}) collective-permute-start(bf16[1,528,128]{2,1,0:T(8,128)(2,1)S(1)} %get-tuple-element.6), channel_id=1, source_target_pairs={{0,8},{4,12},{8,0},{12,4},{16,24},{20,28},{24,16},{28,20},{1,9},{5... | collective-permute-start | bytes 405512 | tf_op jit(solution)/shard_map/ppermute | solution.py:290
  20.2 5.4 %collective-permute-start.4 = (bf16[1,528,128]{2,1,0:T(8,128)(2,1)S(1)}, bf16[1,528,128]{2,1,0:T(8,128)(2,1)S(1)}, u32[]{:S(2)}, u32[]{:S(2)}) collective-permute-start(bf16[1,528,128]{2,1,0:T(8,128)(2,1)S(1)} %get-tuple-element.7), channel_id=1, source_target_pairs={{0,16},{4,20},{8,24},{12,28},{16,0},{20,4},{24,8},{28,12},{1,17},{... | collective-permute-start | bytes 405512 | tf_op jit(solution)/shard_map/ppermute | solution.py:290
  24.9 5.1 %collective-permute-start.3 = (bf16[1,528,128]{2,1,0:T(8,128)(2,1)S(1)}, bf16[1,528,128]{2,1,0:T(8,128)(2,1)S(1)}, u32[]{:S(2)}, u32[]{:S(2)}) collective-permute-start(bf16[1,528,128]{2,1,0:T(8,128)(2,1)S(1)} %add_convert_fusion.1.a0_ref), channel_id=1, source_target_pairs={{0,16},{4,20},{8,24},{12,28},{16,0},{20,4},{24,8},{28,12},{1,17},{... | collective-permute-start | bytes 405512 | tf_op jit(solution)/shard_map/ppermute | solution.py:290
  25.6 7.2 %copy-start.4 = (bf16[2,256,512]{2,1,0:T(8,128)(2,1)S(1)}, bf16[2,256,512]{2,1,0:T(8,128)(2,1)}, u32[]{:S(2)}) copy-start(bf16[2,256,512]{2,1,0:T(8,128)(2,1)} %momentum_ref.1) | copy-start | bytes 1572868
  25.6 5.1 %collective-permute-start.5 = (bf16[1,528,128]{2,1,0:T(8,128)(2,1)S(1)}, bf16[1,528,128]{2,1,0:T(8,128)(2,1)S(1)}, u32[]{:S(2)}, u32[]{:S(2)}) collective-permute-start(bf16[1,528,128]{2,1,0:T(8,128)(2,1)S(1)} %add_convert_fusion.b0_ref), channel_id=1, source_target_pairs={{0,8},{4,12},{8,0},{12,4},{16,24},{20,28},{24,16},{28,20},{1,9},{5... | collective-permute-start | bytes 405512 | tf_op jit(solution)/shard_map/ppermute | solution.py:290
  32.8 4.3 %collective-permute-start.6 = (bf16[1,512,512]{2,1,0:T(8,128)(2,1)S(1)}, bf16[1,512,512]{2,1,0:T(8,128)(2,1)S(1)}, u32[]{:S(2)}, u32[]{:S(2)}) collective-permute-start(bf16[1,512,512]{2,1,0:T(8,128)(2,1)S(1)} %newton_factors.1.factor_ref), channel_id=1, source_target_pairs={{0,4},{4,0},{8,12},{12,8},{16,20},{20,16},{24,28},{28,24},{1,5},{5... | collective-permute-start | bytes 1572872 | tf_op jit(solution)/shard_map/ppermute | solution.py:290
  34.5 1.0 %copy-start.2 = (bf16[2,256,512]{2,1,0:T(8,128)(2,1)S(1)}, bf16[2,256,512]{2,1,0:T(8,128)(2,1)}, u32[]{:S(2)}) copy-start(bf16[2,256,512]{2,1,0:T(8,128)(2,1)} %update_momentum.1.rows_ref) | copy-start | bytes 1572868

commit v2 on v1

v2 whole, which is shorter than its diff:
```python
import functools

import jax
import jax.numpy as jnp
from jax import lax
from jax.experimental import pallas as pl
from jax.experimental.pallas import tpu as pltpu
from jax.sharding import PartitionSpec as P

M = 2048
ITERS = 2

COEF_A = 3.4445
COEF_B = -4.775
COEF_C = 2.0315
DECAY_RATE = 0.95

AXES = ("slab", "group")
VMEM_LIMIT = 24 * 1024 * 1024
HALVES = (
    (((1, 0), (2, 0), (2, 1)), (0, 1)),
    (((3, 0), (3, 1), (3, 2)), (2, 3)),
)
BLOCKS = 4
TAIL = 16


def params(semantics=None, limit=VMEM_LIMIT):
    return pltpu.CompilerParams(vmem_limit_bytes=limit, dimension_semantics=semantics)


def cost(flops, bytes_accessed):
    return pl.CostEstimate(flops=flops, bytes_accessed=bytes_accessed, transcendentals=0)


def whole(memory_space):
    return pl.BlockSpec(memory_space=memory_space)


def squares_kernel(grads_ref, out_ref, held_ref, arrived):
    chunks = arrived.shape[0]
    depth = held_ref.shape[0] // chunks

    def copy(at):
        rows = pl.ds(at * depth, depth)
        return pltpu.make_async_copy(grads_ref.at[rows], held_ref.at[rows], arrived.at[at])

    for at in range(chunks):
        copy(at).start()
    total = jnp.zeros((8, held_ref.shape[1]), jnp.float32)
    for at in range(chunks):
        copy(at).wait()
        values = held_ref[at * depth : (at + 1) * depth, :].astype(jnp.float32)
        total += jnp.sum((values * values).reshape(depth // 8, 8, -1), axis=0)
    lanes = sum(total[:, at : at + 128] for at in range(0, total.shape[1], 128))
    out_ref[...] = jnp.broadcast_to(jnp.sum(lanes, axis=0, keepdims=True), out_ref.shape)


def sum_squares(grads, copies):
    rows, columns = grads.shape[0] * grads.shape[1], grads.shape[2]
    return pl.pallas_call(
        squares_kernel,
        out_shape=jax.ShapeDtypeStruct((copies, 128), jnp.float32),
        in_specs=[whole(pltpu.HBM)],
        out_specs=whole(pltpu.VMEM),
        scratch_shapes=[
            pltpu.VMEM((rows, columns), grads.dtype),
            pltpu.SemaphoreType.DMA((4,)),
        ],
        compiler_params=params(limit=62 * 1024 * 1024),
        cost_estimate=cost(2 * grads.size, 2 * grads.size),
        name="sum_squares",
    )(grads.reshape(rows, columns))


def select_kernel(slot_ref, order_ref, momentum_ref, grads_ref, mine_ref, theirs_ref, arrived):
    half = mine_ref.shape[0]
    core = lax.axis_index("slab") % 2
    copies = []
    for to, (out_ref, side) in enumerate(((mine_ref, core), (theirs_ref, 1 - core))):
        for i in range(half):
            expert = side * half + i
            for kind, source in enumerate(
                (momentum_ref.at[expert], grads_ref.at[slot_ref[0, expert]])
            ):
                copies.append(
                    pltpu.make_async_copy(
                        source, out_ref.at[i, kind], arrived.at[(to * half + i) * 2 + kind]
                    )
                )
    for copy in copies:
        copy.start()
    for copy in copies:
        copy.wait()


def select_rows(grad_slot, order, momentum, grads):
    experts, rows, columns = momentum.shape
    half = experts // 2
    rows_shape = jax.ShapeDtypeStruct((half, 2, rows, columns), momentum.dtype)
    return pl.pallas_call(
        select_kernel,
        out_shape=[rows_shape, rows_shape],
        in_specs=[
            whole(pltpu.SMEM),
            whole(pltpu.HBM),
            whole(pltpu.HBM),
            whole(pltpu.HBM),
        ],
        out_specs=[whole(pltpu.VMEM)] * 2,
        scratch_shapes=[pltpu.SemaphoreType.DMA((4 * half,))],
        compiler_params=params(),
        cost_estimate=cost(0, 8 * momentum.size),
        name="select_rows",
    )(grad_slot, order, momentum, grads)


def fresh_momentum(momentum, gradient, clip):
    return (
        DECAY_RATE * momentum.astype(jnp.float32) + clip * gradient.astype(jnp.float32)
    ).astype(jnp.bfloat16)


def grid_index(shape):
    return (
        lax.broadcasted_iota(jnp.int32, shape, 0),
        lax.broadcasted_iota(jnp.int32, shape, 1),
    )


def clip_kernel(entries, squares_ref, clip_ref):
    total = jnp.sum(squares_ref[...], keepdims=True)
    root_mean = jnp.sqrt(total / entries + 1e-06)
    clip_ref[...] = jnp.broadcast_to(jnp.minimum(1.0, 1.0 / root_mean), clip_ref.shape)


def clip_factor(squares, entries):
    return pl.pallas_call(
        functools.partial(clip_kernel, entries),
        in_specs=[whole(pltpu.VMEM)],
        out_specs=whole(pltpu.VMEM),
        out_shape=jax.ShapeDtypeStruct((8, 128), jnp.float32),
        compiler_params=params(),
        cost_estimate=cost(2**33, 2**23),
        name="clip_factor",
    )(squares)


def gram_kernel(clip_ref, mine_ref, got_ref, pa_ref, pb_ref, rows_ref, gram_ref):
    clip = clip_ref[:1, :1]
    half, _, rows, columns = mine_ref.shape
    size = columns // BLOCKS
    row, column = grid_index((size, size))

    def block(i, j):
        return gram_ref[i * size : (i + 1) * size, j * size : (j + 1) * size]

    for e in range(half):
        for at, source in enumerate((mine_ref, got_ref)):
            rows_ref[e, at] = fresh_momentum(source[e, 0], source[e, 1], clip)
        fresh = rows_ref[e].reshape(2 * rows, columns)
        gram_ref[...] = lax.dot_general(
            fresh, fresh, (((0,), (0,)), ((), ())), preferred_element_type=jnp.float32
        )
        for (lower, (first, second)), out_ref in zip(HALVES, (pa_ref, pb_ref)):
            for at, (i, j) in enumerate(lower):
                out_ref[e, at * size : (at + 1) * size, :] = block(i, j).astype(jnp.bfloat16)
            last = block(second, second)
            shared = jnp.where(column <= row, block(first, first), last)
            out_ref[e, 3 * size : 4 * size, :] = shared.astype(jnp.bfloat16)
            diagonal = jnp.sum(jnp.where(column == row, last, 0.0), axis=0, keepdims=True)
            out_ref[e, 4 * size :, :] = jnp.broadcast_to(diagonal, (TAIL, size)).astype(
                jnp.bfloat16
            )


def packed_grams(clip, mine, got):
    half, _, rows, columns = mine.shape
    size = columns // BLOCKS
    packed = jax.ShapeDtypeStruct((half, 4 * size + TAIL, size), jnp.bfloat16)
    return pl.pallas_call(
        gram_kernel,
        in_specs=[whole(pltpu.VMEM)] * 3,
        out_specs=[whole(pltpu.VMEM)] * 3,
        out_shape=[
            packed,
            packed,
            jax.ShapeDtypeStruct((half, 2, rows, columns), jnp.bfloat16),
        ],
        scratch_shapes=[pltpu.VMEM((columns, columns), jnp.float32)],
        compiler_params=params(),
        cost_estimate=cost(4 * half * rows * columns * columns, 8 * mine.size),
        name="packed_grams",
    )(clip, mine, got)


def momentum_kernel(clip_ref, rows_ref, theirs_ref, out_ref, made_ref, written):
    half = rows_ref.shape[0]
    core = lax.axis_index("slab") % 2
    copies = [
        pltpu.make_async_copy(rows_ref.at[e, 0], out_ref.at[core * half + e], written.at[0, e])
        for e in range(half)
    ]
    for copy in copies:
        copy.start()
    for e in range(half):
        made_ref[e] = fresh_momentum(theirs_ref[e, 0], theirs_ref[e, 1], clip_ref[:1, :1])
        copy = pltpu.make_async_copy(
            made_ref.at[e], out_ref.at[(1 - core) * half + e], written.at[1, e]
        )
        copy.start()
        copies.append(copy)
    for copy in copies:
        copy.wait()


def update_momentum(clip, rows, theirs):
    half, _, depth, columns = rows.shape
    return pl.pallas_call(
        momentum_kernel,
        in_specs=[whole(pltpu.VMEM)] * 3,
        out_specs=whole(pltpu.HBM),
        out_shape=jax.ShapeDtypeStruct((2 * half, depth, columns), jnp.bfloat16),
        scratch_shapes=[
            pltpu.VMEM((half, depth, columns), jnp.bfloat16),
            pltpu.SemaphoreType.DMA((2, half)),
        ],
        compiler_params=params(),
        cost_estimate=cost(3 * rows.size, 6 * rows.size),
        name="update_momentum",
    )(clip, rows, theirs)


def bf16_dot(left, right):
    return jnp.dot(left, right, preferred_element_type=jnp.float32)


def scaled_rows(rows, factor):
    return (jnp.sqrt(jnp.float32(M)) * bf16_dot(rows, factor)).astype(jnp.bfloat16)


def newton_kernel(a0_ref, a1_ref, b0_ref, b1_ref, rows_ref, factor_ref, send_ref, gram_ref):
    e = pl.program_id(0)
    columns = gram_ref.shape[0]
    size = columns // BLOCKS
    row, column = grid_index((size, size))
    for (lower, (first, second)), (x_ref, y_ref) in zip(
        HALVES, ((a0_ref, a1_ref), (b0_ref, b1_ref))
    ):

        def piece(at, end):
            return x_ref[e, at:end, :].astype(jnp.float32) + y_ref[e, at:end, :].astype(
                jnp.float32
            )

        def put(i, j, value):
            gram_ref[i * size : (i + 1) * size, j * size : (j + 1) * size] = value

        for at, (i, j) in enumerate(lower):
            value = piece(at * size, (at + 1) * size)
            put(i, j, value)
            put(j, i, value.T)
        shared = piece(3 * size, 4 * size)
        flipped = shared.T
        diagonal = piece(4 * size, 4 * size + TAIL)[:1, :]
        put(first, first, jnp.where(column <= row, shared, flipped))
        put(
            second,
            second,
            jnp.where(
                column == row, diagonal, jnp.where(column > row, shared, flipped)
            ),
        )
    row, column = grid_index((columns, columns))
    on_diagonal = row == column
    gram = gram_ref[...]
    frob = jnp.sum(jnp.where(on_diagonal, gram, 0.0), keepdims=True) + 1e-06
    current = gram / frob
    product = None
    for iteration in range(ITERS):
        rounded = current.astype(jnp.bfloat16)
        squared = bf16_dot(rounded, rounded)
        poly = (
            jnp.where(on_diagonal, COEF_A, 0.0) + COEF_B * current + COEF_C * squared
        )
        poly_half = poly.astype(jnp.bfloat16)
        if iteration == 0:
            product = poly
        else:
            product = bf16_dot(product.astype(jnp.bfloat16), poly_half)
        if iteration < ITERS - 1:
            halfway = bf16_dot(rounded, poly_half).astype(jnp.bfloat16)
            current = bf16_dot(poly_half, halfway)
    factor = (product / jnp.sqrt(frob)).astype(jnp.bfloat16)
    factor_ref[e] = factor
    send_ref[e] = scaled_rows(rows_ref[e, 1], factor)


def newton_factors(a0, a1, b0, b1, rows):
    half, _, depth, columns = rows.shape
    return pl.pallas_call(
        newton_kernel,
        grid=(half,),
        in_specs=[whole(pltpu.VMEM)] * 5,
        out_specs=[whole(pltpu.VMEM)] * 2,
        out_shape=[
            jax.ShapeDtypeStruct((half, columns, columns), jnp.bfloat16),
            jax.ShapeDtypeStruct((half, depth, columns), jnp.bfloat16),
        ],
        scratch_shapes=[pltpu.VMEM((columns, columns), jnp.float32)],
        compiler_params=params(("arbitrary",)),
        cost_estimate=cost(
            10 * half * columns**3, 2 * (4 * a0.size + half * columns * columns)
        ),
        name="newton_factors",
    )(a0, a1, b0, b1, rows)


def own_kernel(rows_ref, factor_ref, out_ref, made_ref, written):
    half, depth, _ = made_ref.shape
    pieces = written.shape[1]
    size = depth // pieces
    core = lax.axis_index("slab") % 2
    copies = []
    for e in range(half):
        for piece in range(pieces):
            at = pl.ds(piece * size, size)
            made_ref[e, at] = scaled_rows(rows_ref[e, 0, at], factor_ref[e])
            copies.append(
                pltpu.make_async_copy(
                    made_ref.at[e, at], out_ref.at[core * half + e, at], written.at[e, piece]
                )
            )
            copies[-1].start()
    for copy in copies:
        copy.wait()


def update_own(rows, factors):
    half, _, depth, columns = rows.shape
    return pl.pallas_call(
        own_kernel,
        in_specs=[whole(pltpu.VMEM)] * 2,
        out_specs=whole(pltpu.HBM),
        out_shape=jax.ShapeDtypeStruct((2 * half, depth, columns), jnp.bfloat16),
        scratch_shapes=[
            pltpu.VMEM((half, depth, columns), jnp.bfloat16),
            pltpu.SemaphoreType.DMA((half, 2)),
        ],
        compiler_params=params(),
        cost_estimate=cost(2 * half * depth * columns * columns, 6 * half * depth * columns),
        name="update_own",
    )(rows, factors)


def other_kernel(got_ref, update_ref, out_ref, written):
    half = got_ref.shape[0]
    other = 1 - lax.axis_index("slab") % 2
    copy = pltpu.make_async_copy(got_ref, out_ref.at[pl.ds(other * half, half)], written)
    copy.start()
    copy.wait()


def update_other(got, update):
    return pl.pallas_call(
        other_kernel,
        in_specs=[whole(pltpu.VMEM), whole(pltpu.HBM)],
        out_specs=whole(pltpu.HBM),
        out_shape=jax.ShapeDtypeStruct(update.shape, update.dtype),
        scratch_shapes=[pltpu.SemaphoreType.DMA],
        input_output_aliases={1: 0},
        compiler_params=params(),
        cost_estimate=cost(0, 4 * got.size),
        name="update_other",
    )(got, update)


def add_rounded(left, right):
    return (left.astype(jnp.float32) + right.astype(jnp.float32)).astype(jnp.bfloat16)


def on_device(grads, grad_slot, momentum):
    slab_count = lax.axis_size("slab")
    devices = slab_count * lax.axis_size("group")

    def swap(value, bit):
        return lax.ppermute(value, "slab", [(i, i ^ bit) for i in range(slab_count)])

    partial = sum_squares(grads, devices)
    squares = lax.all_to_all(partial, AXES, 0, 0, tiled=True)
    mine, theirs = select_rows(grad_slot, partial, momentum, grads)
    got = swap(theirs, 1)
    clip = clip_factor(squares, grads.size * devices)
    a, b, rows = packed_grams(clip, mine, got)
    bits = []
    while 2 << len(bits) < slab_count:
        bits.append(2 << len(bits))
    turned = bits[len(bits) // 2 :] + bits[: len(bits) // 2]
    fresh = update_momentum(clip, rows, theirs)
    for step, (bit_a, bit_b) in enumerate(zip(bits, turned)):
        a1, b1 = swap(a, bit_a), swap(b, bit_b)
        if step < len(bits) - 1:
            a, b = add_rounded(a, a1), add_rounded(b, b1)
        if step == 0:
            a, b, fresh = lax.optimization_barrier((a, b, fresh))
    factors, send = newton_factors(a, a1, b, b1, rows)
    update = update_other(swap(send, 1), update_own(rows, factors))
    return (fresh, update)


def solution(mesh):
    in_specs = (P("group", "slab", None), P("group", None), P("group", "slab", None))
    out_specs = (P("group", "slab", None), P("group", "slab", None))
    return jax.shard_map(
        on_device, mesh=mesh, in_specs=in_specs, out_specs=out_specs, check_vma=False
    )
```

time: 38.9 us -> 33.7 us (0.87)
  local copies, waits for them, and re-layouts: 3.78 us -> 1.05 us
  waiting for transfers between devices: 14.4 us -> 12.6 us
  Pallas kernels: 8.59 us -> 7.99 us
    unnamed x12 -> x8, local copies, waits for them, and re-layouts: 3.78 us -> 1.05 us
    pallas_call x5 -> x7, Pallas kernels: 7.94 us -> 6.17 us  [the longest x1 2.24 us: newton_factors(): pl.pallas_call(newton_kernel, grid=(half,), in_specs=[whole(pltpu.VMEM)]...]
    all_to_all x1, waiting for transfers between devices: 6.35 us -> 5.02 us  [on_device(): squares = lax.all_to_all(partial, AXES, 0, 0, tiled=True)]
    pallas_call x1, Pallas kernels: 0.65 us -> 1.81 us  [sum_squares(): pl.pallas_call(squares_kernel, out_shape=jax.ShapeDtypeStruct((copies, 12...]
    ppermute x7 -> x6, waiting for transfers between devices: 8.08 us -> 7.58 us  [swap(): lax.ppermute(value, 'slab', [(i, i ^ bit) for i in range(slab_count)])]
    ppermute x7 -> x6, starting transfers between devices: 3.65 us -> 3.66 us  [swap(): lax.ppermute(value, 'slab', [(i, i ^ bit) for i in range(slab_count)])]
  transfers between devices with their start and end apart: 8 -> 7, of which waited for: 4 -> 6; matrix products, arithmetic and copies ran while one was open for 0% -> 0% of each run, Pallas kernels for 10% -> 8%
where the time goes in v2:
time: 33.7 us; the launch traced here: 33.5 us
  waiting for transfers between devices  12.6 us (37%)
  starting transfers between devices  11 us (33%)
  Pallas kernels  7.99 us (24%)
  local copies, waits for them, and re-layouts  1.05 us (3%)
  between operations  0.77 us (2%)
    ppermute x6, waiting for transfers between devices, swap(): lax.ppermute(value, 'slab', [(i, i ^ bit) for i in range(slab_count)])  7.58 us
    all_to_all x1, starting transfers between devices, on_device(): squares = lax.all_to_all(partial, AXES, 0, 0, tiled=True)  7.3 us
    all_to_all x1, waiting for transfers between devices, on_device(): squares = lax.all_to_all(partial, AXES, 0, 0, tiled=True)  5.02 us
    ppermute x6, starting transfers between devices, swap(): lax.ppermute(value, 'slab', [(i, i ^ bit) for i in range(slab_count)])  3.66 us
    pallas_call x1, Pallas kernels, newton_factors(): pl.pallas_call(newton_kernel, grid=(half,), in_specs=[whole(pltpu.VMEM)]...  2.24 us
    pallas_call x1, Pallas kernels, sum_squares(): pl.pallas_call(squares_kernel, out_shape=jax.ShapeDtypeStruct((copies, 12...  1.81 us
    unnamed x8, local copies, waits for them, and re-layouts  1.05 us
    pallas_call x1, Pallas kernels, update_own(): pl.pallas_call(own_kernel, in_specs=[whole(pltpu.VMEM)] * 2, out_specs=wh...  0.99 us
  transfers between devices with their start and end apart: 7, of which 6 were waited for; matrix products, arithmetic and copies ran while one was open for 0% of the time, Pallas kernels for 8%

profile of v2, /device:TPU:0, one launch (start us, length us, event | category | flops | bytes accessed | tf_op | source)
XLA Modules:
  0.0 33.5 jit_solution(9840270955763612603)
XLA Ops:
  0.6 0.0 copy-start
  0.6 1.8 %sum_squares.1.order_ref = f32[32,128]{1,0:T(8,128)} custom-call(bf16[512,512]{1,0:T(8,128)(2,1)} %bitcast.5), custom_call_target="tpu_custom_call" | custom-call | flops 524288 | bytes 524288 | tf_op jit(solution)/shard_map/sum_squares/pallas_call | solution.py:61
  2.5 0.0 copy-start.2
  2.5 0.0 copy-start.3
  2.5 7.3 %all-to-all-start = ((f32[32,1,128]{2,1,0:T(1,128)}), f32[32,1,128]{2,1,0:T(1,128)S(1)}, u32[]{:S(2)}, u32[]{:S(2)}) async-start(f32[32,1,128]{2,1,0:T(1,128)} %bitcast.6), calls=%async_computation | async-start | bytes 32768 | tf_op jit(solution)/shard_map/all_to_all | solution.py:390
  9.8 0.0 copy-done
  9.8 0.0 copy-done.2
  9.8 0.0 copy-done.3
  9.8 0.0 copy-start.1
  9.8 1.0 %copy-done.1 = bf16[2,256,512]{2,1,0:T(8,128)(2,1)S(1)} copy-done((bf16[2,256,512]{2,1,0:T(8,128)(2,1)S(1)}, bf16[2,256,512]{2,1,0:T(8,128)(2,1)}, u32[]{:S(2)}) %copy-start.1) | copy-done | bytes 524312
  10.9 0.7 %select_rows.1 = (bf16[1,2,256,512]{3,2,1,0:T(8,128)(2,1)S(1)}, bf16[1,2,256,512]{3,2,1,0:T(8,128)(2,1)S(1)}) custom-call(s32[1,2]{1,0:T(1,128)S(1)} %copy-done.3, f32[32,128]{1,0:T(8,128)S(1)} %copy-done.2, bf16[2,256,512]{2,1,0:T(8,128)(2,1)S(1)} %copy-done.1, bf16[2,256,512]{2,1,0:T(8,128)(2,1)S(1)} %copy-done), custom_call_target="tpu_custom_call" | custom-call | bytes 2097152 | tf_op jit(solution)/shard_map/select_rows/pallas_call | solution.py:101
  11.6 0.3 collective-permute-start
  11.9 5.0 %all-to-all-done = f32[32,1,128]{2,1,0:T(1,128)S(1)} async-done(((f32[32,1,128]{2,1,0:T(1,128)}), f32[32,1,128]{2,1,0:T(1,128)S(1)}, u32[]{:S(2)}, u32[]{:S(2)}) %all-to-all-start) | async-done | bytes 16416 | tf_op jit(solution)/shard_map/all_to_all | solution.py:390
  16.9 0.1 clip_factor.1.clip_ref
  17.0 0.0 collective-permute-done.got_ref
  17.0 0.6 %packed_grams.1 = (bf16[1,528,128]{2,1,0:T(8,128)(2,1)S(1)}, bf16[1,528,128]{2,1,0:T(8,128)(2,1)S(1)}, bf16[1,2,256,512]{3,2,1,0:T(8,128)(2,1)S(1)}) custom-call(f32[8,128]{1,0:T(8,128)S(1)} %clip_factor.1.clip_ref, bf16[1,2,256,512]{3,2,1,0:T(8,128)(2,1)S(1)} %get-tuple-element.12.mine_ref, bf16[1,2,256,512]{3,2,1,0:T(8,128)(2,1)S(1)} %collective-permute-done.got_ref), custom_call_target="tpu_custom_call" | custom-call | flops 268435456 | bytes 2097152 | tf_op jit(solution)/shard_map/packed_grams/pallas_call | solution.py:181
  17.6 0.6 %collective-permute-start.1 = (bf16[1,528,128]{2,1,0:T(8,128)(2,1)S(1)}, bf16[1,528,128]{2,1,0:T(8,128)(2,1)S(1)}, u32[]{:S(2)}, u32[]{:S(2)}) collective-permute-start(bf16[1,528,128]{2,1,0:T(8,128)(2,1)S(1)} %get-tuple-element.14), channel_id=1, source_target_pairs={{0,8},{4,12},{8,0},{12,4},{16,24},{20,28},{24,16},{28,20},{1,9},{5... | collective-permute-start | bytes 405512 | tf_op jit(solution)/shard_map/ppermute | solution.py:387
  18.2 0.5 %collective-permute-start.2 = (bf16[1,528,128]{2,1,0:T(8,128)(2,1)S(1)}, bf16[1,528,128]{2,1,0:T(8,128)(2,1)S(1)}, u32[]{:S(2)}, u32[]{:S(2)}) collective-permute-start(bf16[1,528,128]{2,1,0:T(8,128)(2,1)S(1)} %get-tuple-element.15), channel_id=1, source_target_pairs={{0,16},{4,20},{8,24},{12,28},{16,0},{20,4},{24,8},{28,12},{1,17},{... | collective-permute-start | bytes 405512 | tf_op jit(solution)/shard_map/ppermute | solution.py:387
  18.8 0.9 %update_momentum.1 = bf16[2,256,512]{2,1,0:T(8,128)(2,1)} custom-call(f32[8,128]{1,0:T(8,128)S(1)} %clip_factor.1.clip_ref, bf16[1,2,256,512]{3,2,1,0:T(8,128)(2,1)S(1)} %get-tuple-element.16.rows_ref, bf16[1,2,256,512]{3,2,1,0:T(8,128)(2,1)S(1)} %get-tuple-element.13.theirs_ref), custom_call_target="tpu_custom_call" | custom-call | flops 786432 | bytes 1572864 | tf_op jit(solution)/shard_map/update_momentum/pallas_call | solution.py:219
  19.7 3.2 %collective-permute-done.1 = bf16[1,528,128]{2,1,0:T(8,128)(2,1)S(1)} collective-permute-done((bf16[1,528,128]{2,1,0:T(8,128)(2,1)S(1)}, bf16[1,528,128]{2,1,0:T(8,128)(2,1)S(1)}, u32[]{:S(2)}, u32[]{:S(2)}) %collective-permute-start.1) | collective-permute-done | bytes 135200 | tf_op jit(solution)/shard_map/ppermute | solution.py:387
  23.0 0.3 collective-permute-done.2
  23.3 0.6 %collective-permute-start.3 = (bf16[1,528,128]{2,1,0:T(8,128)(2,1)S(1)}, bf16[1,528,128]{2,1,0:T(8,128)(2,1)S(1)}, u32[]{:S(2)}, u32[]{:S(2)}) collective-permute-start(bf16[1,528,128]{2,1,0:T(8,128)(2,1)S(1)} %add_convert_fusion.1.a0_ref), channel_id=1, source_target_pairs={{0,16},{4,20},{8,24},{12,28},{16,0},{20,4},{24,8},{28,12},{1,17},{... | collective-permute-start | bytes 405512 | tf_op jit(solution)/shard_map/ppermute | solution.py:387
  23.9 1.5 %collective-permute-start.4 = (bf16[1,528,128]{2,1,0:T(8,128)(2,1)S(1)}, bf16[1,528,128]{2,1,0:T(8,128)(2,1)S(1)}, u32[]{:S(2)}, u32[]{:S(2)}) collective-permute-start(bf16[1,528,128]{2,1,0:T(8,128)(2,1)S(1)} %add_convert_fusion.b0_ref), channel_id=1, source_target_pairs={{0,8},{4,12},{8,0},{12,4},{16,24},{20,28},{24,16},{28,20},{1,9},{5... | collective-permute-start | bytes 405512 | tf_op jit(solution)/shard_map/ppermute | solution.py:387
  25.4 3.0 %collective-permute-done.3.a1_ref = bf16[1,528,128]{2,1,0:T(8,128)(2,1)S(1)} collective-permute-done((bf16[1,528,128]{2,1,0:T(8,128)(2,1)S(1)}, bf16[1,528,128]{2,1,0:T(8,128)(2,1)S(1)}, u32[]{:S(2)}, u32[]{:S(2)}) %collective-permute-start.3) | collective-permute-done | bytes 135200 | tf_op jit(solution)/shard_map/ppermute | solution.py:387
  28.4 0.5 %collective-permute-done.4.b1_ref = bf16[1,528,128]{2,1,0:T(8,128)(2,1)S(1)} collective-permute-done((bf16[1,528,128]{2,1,0:T(8,128)(2,1)S(1)}, bf16[1,528,128]{2,1,0:T(8,128)(2,1)S(1)}, u32[]{:S(2)}, u32[]{:S(2)}) %collective-permute-start.4) | collective-permute-done | bytes 135200 | tf_op jit(solution)/shard_map/ppermute | solution.py:387
  28.9 2.2 %newton_factors.1 = (bf16[1,512,512]{2,1,0:T(8,128)(2,1)S(1)}, bf16[1,256,512]{2,1,0:T(8,128)(2,1)S(1)}) custom-call(bf16[1,528,128]{2,1,0:T(8,128)(2,1)S(1)} %add_convert_fusion.1.a0_ref, bf16[1,528,128]{2,1,0:T(8,128)(2,1)S(1)} %collective-permute-done.3.a1_ref, bf16[1,528,128]{2,1,0:T(8,128)(2,1)S(1)} %add_convert_fusion.b0_ref, ...), custom_call_target="tpu_custom_call" | custom-call | flops 1342177280 | bytes 1064960 | tf_op jit(solution)/shard_map/newton_factors/pallas_call | solution.py:301
  31.1 0.1 collective-permute-start.5
  31.2 1.0 %update_own.1.update_ref = bf16[2,256,512]{2,1,0:T(8,128)(2,1)} custom-call(bf16[1,2,256,512]{3,2,1,0:T(8,128)(2,1)S(1)} %get-tuple-element.16.rows_ref, bf16[1,512,512]{2,1,0:T(8,128)(2,1)S(1)} %get-tuple-element.21.factor_ref), custom_call_target="tpu_custom_call" | custom-call | flops 134217728 | bytes 786432 | tf_op jit(solution)/shard_map/update_own/pallas_call | solution.py:341
  32.2 0.5 %collective-permute-done.5.got_ref = bf16[1,256,512]{2,1,0:T(8,128)(2,1)S(1)} collective-permute-done((bf16[1,256,512]{2,1,0:T(8,128)(2,1)S(1)}, bf16[1,256,512]{2,1,0:T(8,128)(2,1)S(1)}, u32[]{:S(2)}, u32[]{:S(2)}) %collective-permute-start.5) | collective-permute-done | bytes 262176 | tf_op jit(solution)/shard_map/ppermute | solution.py:387
  32.7 0.7 %update_other.1 = bf16[2,256,512]{2,1,0:T(8,128)(2,1)} custom-call(bf16[1,256,512]{2,1,0:T(8,128)(2,1)S(1)} %collective-permute-done.5.got_ref, bf16[2,256,512]{2,1,0:T(8,128)(2,1)} %update_own.1.update_ref), custom_call_target="tpu_custom_call", output_to_operand_aliasing={{}: (1, {})} | custom-call | bytes 524288 | tf_op jit(solution)/shard_map/update_other/pallas_call | solution.py:365
  (2 shorter events, 0.1 us)
Async XLA Ops:
  0.6 9.2 %copy-start = (bf16[2,256,512]{2,1,0:T(8,128)(2,1)S(1)}, bf16[2,256,512]{2,1,0:T(8,128)(2,1)}, u32[]{:S(2)}) copy-start(bf16[2,256,512]{2,1,0:T(8,128)(2,1)} %grads_ref.1) | copy-start | bytes 1572868
  2.5 7.3 %copy-start.2 = (f32[32,128]{1,0:T(8,128)S(1)}, f32[32,128]{1,0:T(8,128)}, u32[]{:S(2)}) copy-start(f32[32,128]{1,0:T(8,128)} %sum_squares.1.order_ref) | copy-start | bytes 49156
  2.5 7.3 %copy-start.3 = (s32[1,2]{1,0:T(1,128)S(1)}, s32[1,2]{1,0:T(1,128)}, u32[]{:S(2)}) copy-start(s32[1,2]{1,0:T(1,128)} %slot_ref.1) | copy-start | bytes 28
  2.5 14.4 %all-to-all-start = ((f32[32,1,128]{2,1,0:T(1,128)}), f32[32,1,128]{2,1,0:T(1,128)S(1)}, u32[]{:S(2)}, u32[]{:S(2)}) async-start(f32[32,1,128]{2,1,0:T(1,128)} %bitcast.6), calls=%async_computation | async-start | bytes 32768 | tf_op jit(solution)/shard_map/all_to_all | solution.py:390
  9.8 1.0 %copy-start.1 = (bf16[2,256,512]{2,1,0:T(8,128)(2,1)S(1)}, bf16[2,256,512]{2,1,0:T(8,128)(2,1)}, u32[]{:S(2)}) copy-start(bf16[2,256,512]{2,1,0:T(8,128)(2,1)} %momentum_ref.1) | copy-start | bytes 1572868
  11.6 5.5 %collective-permute-start = (bf16[1,2,256,512]{3,2,1,0:T(8,128)(2,1)S(1)}, bf16[1,2,256,512]{3,2,1,0:T(8,128)(2,1)S(1)}, u32[]{:S(2)}, u32[]{:S(2)}) collective-permute-start(bf16[1,2,256,512]{3,2,1,0:T(8,128)(2,1)S(1)} %get-tuple-element.13.theirs_ref), channel_id=1, source_target_pairs={{0,4},{4,0},{8,12},{12,8},{16,20},{20,16},{24,28},{28,24},{1,5},{5... | collective-permute-start | bytes 1572872 | tf_op jit(solution)/shard_map/ppermute | solution.py:387
  17.6 5.3 %collective-permute-start.1 = (bf16[1,528,128]{2,1,0:T(8,128)(2,1)S(1)}, bf16[1,528,128]{2,1,0:T(8,128)(2,1)S(1)}, u32[]{:S(2)}, u32[]{:S(2)}) collective-permute-start(bf16[1,528,128]{2,1,0:T(8,128)(2,1)S(1)} %get-tuple-element.14), channel_id=1, source_target_pairs={{0,8},{4,12},{8,0},{12,4},{16,24},{20,28},{24,16},{28,20},{1,9},{5... | collective-permute-start | bytes 405512 | tf_op jit(solution)/shard_map/ppermute | solution.py:387
  18.2 5.0 %collective-permute-start.2 = (bf16[1,528,128]{2,1,0:T(8,128)(2,1)S(1)}, bf16[1,528,128]{2,1,0:T(8,128)(2,1)S(1)}, u32[]{:S(2)}, u32[]{:S(2)}) collective-permute-start(bf16[1,528,128]{2,1,0:T(8,128)(2,1)S(1)} %get-tuple-element.15), channel_id=1, source_target_pairs={{0,16},{4,20},{8,24},{12,28},{16,0},{20,4},{24,8},{28,12},{1,17},{... | collective-permute-start | bytes 405512 | tf_op jit(solution)/shard_map/ppermute | solution.py:387
  23.3 5.1 %collective-permute-start.3 = (bf16[1,528,128]{2,1,0:T(8,128)(2,1)S(1)}, bf16[1,528,128]{2,1,0:T(8,128)(2,1)S(1)}, u32[]{:S(2)}, u32[]{:S(2)}) collective-permute-start(bf16[1,528,128]{2,1,0:T(8,128)(2,1)S(1)} %add_convert_fusion.1.a0_ref), channel_id=1, source_target_pairs={{0,16},{4,20},{8,24},{12,28},{16,0},{20,4},{24,8},{28,12},{1,17},{... | collective-permute-start | bytes 405512 | tf_op jit(solution)/shard_map/ppermute | solution.py:387
  23.9 5.0 %collective-permute-start.4 = (bf16[1,528,128]{2,1,0:T(8,128)(2,1)S(1)}, bf16[1,528,128]{2,1,0:T(8,128)(2,1)S(1)}, u32[]{:S(2)}, u32[]{:S(2)}) collective-permute-start(bf16[1,528,128]{2,1,0:T(8,128)(2,1)S(1)} %add_convert_fusion.b0_ref), channel_id=1, source_target_pairs={{0,8},{4,12},{8,0},{12,4},{16,24},{20,28},{24,16},{28,20},{1,9},{5... | collective-permute-start | bytes 405512 | tf_op jit(solution)/shard_map/ppermute | solution.py:387
  31.1 1.6 %collective-permute-start.5 = (bf16[1,256,512]{2,1,0:T(8,128)(2,1)S(1)}, bf16[1,256,512]{2,1,0:T(8,128)(2,1)S(1)}, u32[]{:S(2)}, u32[]{:S(2)}) collective-permute-start(bf16[1,256,512]{2,1,0:T(8,128)(2,1)S(1)} %get-tuple-element.20), channel_id=1, source_target_pairs={{0,4},{4,0},{8,12},{12,8},{16,20},{20,16},{24,28},{28,24},{1,5},{5... | collective-permute-start | bytes 786440 | tf_op jit(solution)/shard_map/ppermute | solution.py:387

commit v3 on v2

--- a/solution.py
+++ b/solution.py
@@ -37,21 +37,9 @@
     return pl.BlockSpec(memory_space=memory_space)
 
 
-def squares_kernel(grads_ref, out_ref, held_ref, arrived):
-    chunks = arrived.shape[0]
-    depth = held_ref.shape[0] // chunks
-
-    def copy(at):
-        rows = pl.ds(at * depth, depth)
-        return pltpu.make_async_copy(grads_ref.at[rows], held_ref.at[rows], arrived.at[at])
-
-    for at in range(chunks):
-        copy(at).start()
-    total = jnp.zeros((8, held_ref.shape[1]), jnp.float32)
-    for at in range(chunks):
-        copy(at).wait()
-        values = held_ref[at * depth : (at + 1) * depth, :].astype(jnp.float32)
-        total += jnp.sum((values * values).reshape(depth // 8, 8, -1), axis=0)
+def squares_kernel(grads_ref, out_ref):
+    values = grads_ref[...].astype(jnp.float32)
+    total = jnp.sum((values * values).reshape(values.shape[0] // 8, 8, -1), axis=0)
     lanes = sum(total[:, at : at + 128] for at in range(0, total.shape[1], 128))
     out_ref[...] = jnp.broadcast_to(jnp.sum(lanes, axis=0, keepdims=True), out_ref.shape)
 
@@ -61,13 +49,9 @@
     return pl.pallas_call(
         squares_kernel,
         out_shape=jax.ShapeDtypeStruct((copies, 128), jnp.float32),
-        in_specs=[whole(pltpu.HBM)],
+        in_specs=[whole(pltpu.VMEM)],
         out_specs=whole(pltpu.VMEM),
-        scratch_shapes=[
-            pltpu.VMEM((rows, columns), grads.dtype),
-            pltpu.SemaphoreType.DMA((4,)),
-        ],
-        compiler_params=params(limit=62 * 1024 * 1024),
+        compiler_params=params(),
         cost_estimate=cost(2 * grads.size, 2 * grads.size),
         name="sum_squares",
     )(grads.reshape(rows, columns))
@@ -159,9 +143,16 @@
         for at, source in enumerate((mine_ref, got_ref)):
             rows_ref[e, at] = fresh_momentum(source[e, 0], source[e, 1], clip)
         fresh = rows_ref[e].reshape(2 * rows, columns)
-        gram_ref[...] = lax.dot_general(
-            fresh, fresh, (((0,), (0,)), ((), ())), preferred_element_type=jnp.float32
-        )
+        middle = columns // 2
+        for rows_at, columns_at in ((0, 0), (middle, 0), (middle, middle)):
+            gram_ref[rows_at : rows_at + middle, columns_at : columns_at + middle] = (
+                lax.dot_general(
+                    fresh[:, rows_at : rows_at + middle],
+                    fresh[:, columns_at : columns_at + middle],
+                    (((0,), (0,)), ((), ())),
+                    preferred_element_type=jnp.float32,
+                )
+            )
         for (lower, (first, second)), out_ref in zip(HALVES, (pa_ref, pb_ref)):
             for at, (i, j) in enumerate(lower):
                 out_ref[e, at * size : (at + 1) * size, :] = block(i, j).astype(jnp.bfloat16)
@@ -239,59 +230,84 @@
     return (jnp.sqrt(jnp.float32(M)) * bf16_dot(rows, factor)).astype(jnp.bfloat16)
 
 
+def lower_product(left, right):
+    half = left.shape[0] // 2
+    return (
+        bf16_dot(left[:half], right[:, :half]),
+        bf16_dot(left[half:], right[:, :half]),
+        bf16_dot(left[half:], right[:, half:]),
+    )
+
+
+def mirrored(parts):
+    upper, corner, lower = (part.astype(jnp.bfloat16) for part in parts)
+    return jnp.concatenate(
+        [
+            jnp.concatenate([upper, corner.T], axis=1),
+            jnp.concatenate([corner, lower], axis=1),
+        ],
+        axis=0,
+    )
+
+
 def newton_kernel(a0_ref, a1_ref, b0_ref, b1_ref, rows_ref, factor_ref, send_ref, gram_ref):
     e = pl.program_id(0)
     columns = gram_ref.shape[0]
     size = columns // BLOCKS
     row, column = grid_index((size, size))
-    for (lower, (first, second)), (x_ref, y_ref) in zip(
-        HALVES, ((a0_ref, a1_ref), (b0_ref, b1_ref))
-    ):
-
-        def piece(at, end):
-            return x_ref[e, at:end, :].astype(jnp.float32) + y_ref[e, at:end, :].astype(
-                jnp.float32
-            )
-
-        def put(i, j, value):
-            gram_ref[i * size : (i + 1) * size, j * size : (j + 1) * size] = value
-
-        for at, (i, j) in enumerate(lower):
-            value = piece(at * size, (at + 1) * size)
+    packs = ((a0_ref, a1_ref), (b0_ref, b1_ref))
+
+    def piece(pack, at, end):
+        return sum(ref[e, at:end, :].astype(jnp.float32) for ref in pack)
+
+    shared = [piece(pack, 3 * size, 4 * size) for pack in packs]
+    diagonal = [piece(pack, 4 * size, 4 * size + TAIL)[:1, :] for pack in packs]
+    trace = sum(jnp.sum(jnp.where(column == row, value, 0.0), keepdims=True) for value in shared)
+    trace += sum(jnp.sum(value, keepdims=True) for value in diagonal)
+    frob = trace + 1e-06
+    scale = 1.0 / frob
+
+    def put(i, j, value):
+        gram_ref[i * size : (i + 1) * size, j * size : (j + 1) * size] = value
+
+    for at, (lower, (first, second)) in enumerate(HALVES):
+        for k, (i, j) in enumerate(lower):
+            value = scale * piece(packs[at], k * size, (k + 1) * size)
             put(i, j, value)
-            put(j, i, value.T)
-        shared = piece(3 * size, 4 * size)
-        flipped = shared.T
-        diagonal = piece(4 * size, 4 * size + TAIL)[:1, :]
-        put(first, first, jnp.where(column <= row, shared, flipped))
+            if i // 2 == j // 2:
+                put(j, i, value.T)
+        value = scale * shared[at]
+        flipped = value.T
+        put(first, first, jnp.where(column <= row, value, flipped))
         put(
             second,
             second,
             jnp.where(
-                column == row, diagonal, jnp.where(column > row, shared, flipped)
+                column == row,
+                scale * diagonal[at],
+                jnp.where(column > row, value, flipped),
             ),
         )
-    row, column = grid_index((columns, columns))
-    on_diagonal = row == column
-    gram = gram_ref[...]
-    frob = jnp.sum(jnp.where(on_diagonal, gram, 0.0), keepdims=True) + 1e-06
-    current = gram / frob
-    product = None
+    half = columns // 2
+    row, column = grid_index((half, half))
+    identity = jnp.where(row == column, COEF_A, 0.0)
+    current = (gram_ref[:half, :half], gram_ref[half:, :half], gram_ref[half:, half:])
     for iteration in range(ITERS):
-        rounded = current.astype(jnp.bfloat16)
-        squared = bf16_dot(rounded, rounded)
-        poly = (
-            jnp.where(on_diagonal, COEF_A, 0.0) + COEF_B * current + COEF_C * squared
-        )
-        poly_half = poly.astype(jnp.bfloat16)
+        rounded = mirrored(current)
+        squared = lower_product(rounded, rounded)
+        poly = [COEF_B * x + COEF_C * y for x, y in zip(current, squared)]
+        poly_half = mirrored((identity + poly[0], poly[1], identity + poly[2]))
         if iteration == 0:
-            product = poly
+            product = poly_half
         else:
-            product = bf16_dot(product.astype(jnp.bfloat16), poly_half)
+            product = lower_product(product, poly_half)
+            if iteration < ITERS - 1:
+                product = mirrored(product)
         if iteration < ITERS - 1:
-            halfway = bf16_dot(rounded, poly_half).astype(jnp.bfloat16)
-            current = bf16_dot(poly_half, halfway)
-    factor = (product / jnp.sqrt(frob)).astype(jnp.bfloat16)
+            halfway = mirrored(lower_product(rounded, poly_half))
+            current = lower_product(poly_half, halfway)
+    scale = lax.rsqrt(frob)
+    factor = mirrored([part * scale for part in product])
     factor_ref[e] = factor
     send_ref[e] = scaled_rows(rows_ref[e, 1], factor)
 
@@ -383,8 +399,10 @@
     slab_count = lax.axis_size("slab")
     devices = slab_count * lax.axis_size("group")
 
-    def swap(value, bit):
-        return lax.ppermute(value, "slab", [(i, i ^ bit) for i in range(slab_count)])
+    def swap(value, bit, odd_bit=None):
+        odd_bit = odd_bit or bit
+        pairs = [(i, i ^ (odd_bit if i % 2 else bit)) for i in range(slab_count)]
+        return lax.ppermute(value, "slab", pairs)
 
     partial = sum_squares(grads, devices)
     squares = lax.all_to_all(partial, AXES, 0, 0, tiled=True)
@@ -402,7 +420,7 @@
         if step < len(bits) - 1:
             a, b = add_rounded(a, a1), add_rounded(b, b1)
         if step == 0:
-            a, b, fresh = lax.optimization_barrier((a, b, fresh))
+            a, fresh = lax.optimization_barrier((a, fresh))
     factors, send = newton_factors(a, a1, b, b1, rows)
     update = update_other(swap(send, 1), update_own(rows, factors))
     return (fresh, update)

time: 33.7 us -> 33 us (0.979)
  Pallas kernels: 7.99 us -> 6.45 us
  local copies, waits for them, and re-layouts: 1.05 us -> 2.08 us
    pallas_call x1, Pallas kernels: 1.81 us -> 0.65 us  [sum_squares(): pl.pallas_call(squares_kernel, out_shape=jax.ShapeDtypeStruct((copies, 12...]
    unnamed x8, local copies, waits for them, and re-layouts: 1.05 us -> 2.08 us
  transfers between devices with their start and end apart: 7 -> 7, of which waited for: 6 -> 5; matrix products, arithmetic and copies ran while one was open for 0% -> 0% of each run, Pallas kernels for 8% -> 8%
where the time goes in v3:
time: 33 us; the launch traced here: 32.7 us
  waiting for transfers between devices  12.7 us (38%)
  starting transfers between devices  10.7 us (32%)
  Pallas kernels  6.45 us (20%)
  local copies, waits for them, and re-layouts  2.08 us (6%)
  between operations  0.74 us (2%)
    ppermute x6, waiting for transfers between devices, swap(): return lax.ppermute(value, 'slab', pairs)  7.71 us
    all_to_all x1, starting transfers between devices, on_device(): squares = lax.all_to_all(partial, AXES, 0, 0, tiled=True)  7.3 us
    all_to_all x1, waiting for transfers between devices, on_device(): squares = lax.all_to_all(partial, AXES, 0, 0, tiled=True)  5.03 us
    ppermute x6, starting transfers between devices, swap(): return lax.ppermute(value, 'slab', pairs)  3.36 us
    unnamed x8, local copies, waits for them, and re-layouts  2.08 us
    pallas_call x1, Pallas kernels, newton_factors(): pl.pallas_call(newton_kernel, grid=(half,), in_specs=[whole(pltpu.VMEM)]...  1.93 us
    pallas_call x1, Pallas kernels, update_own(): pl.pallas_call(own_kernel, in_specs=[whole(pltpu.VMEM)] * 2, out_specs=wh...  0.99 us
    pallas_call x1, Pallas kernels, update_momentum(): pl.pallas_call(momentum_kernel, in_specs=[whole(pltpu.VMEM)] * 3, out_spe...  0.89 us
  transfers between devices with their start and end apart: 7, of which 5 were waited for; matrix products, arithmetic and copies ran while one was open for 0% of the time, Pallas kernels for 8%

profile of v3, /device:TPU:0, one launch (start us, length us, event | category | flops | bytes accessed | tf_op | source)
XLA Modules:
  0.0 32.7 jit_solution(16155651654913886040)
XLA Ops:
  0.6 0.0 copy-start
  0.6 1.0 %copy-done = bf16[2,256,512]{2,1,0:T(8,128)(2,1)S(1)} copy-done((bf16[2,256,512]{2,1,0:T(8,128)(2,1)S(1)}, bf16[2,256,512]{2,1,0:T(8,128)(2,1)}, u32[]{:S(2)}) %copy-start) | copy-done | bytes 524312
  1.7 0.0 copy-start.1
  1.7 0.7 %sum_squares.1.order_ref = f32[32,128]{1,0:T(8,128)} custom-call(bf16[512,512]{1,0:T(8,128)(2,1)S(1)} %bitcast.5), custom_call_target="tpu_custom_call" | custom-call | flops 524288 | bytes 524288 | tf_op jit(solution)/shard_map/sum_squares/pallas_call | solution.py:49
  2.3 0.0 copy-start.3
  2.3 7.3 %all-to-all-start = ((f32[32,1,128]{2,1,0:T(1,128)}), f32[32,1,128]{2,1,0:T(1,128)S(1)}, u32[]{:S(2)}, u32[]{:S(2)}) async-start(f32[32,1,128]{2,1,0:T(1,128)} %bitcast.2), calls=%async_computation | async-start | bytes 32768 | tf_op jit(solution)/shard_map/all_to_all | solution.py:408
  9.6 0.0 copy-done.1
  9.6 0.0 copy-done.3
  9.7 0.0 copy-start.2
  9.7 1.0 %copy-done.2 = bf16[2,256,512]{2,1,0:T(8,128)(2,1)S(1)} copy-done((bf16[2,256,512]{2,1,0:T(8,128)(2,1)S(1)}, bf16[2,256,512]{2,1,0:T(8,128)(2,1)}, u32[]{:S(2)}) %copy-start.2) | copy-done | bytes 524312
  10.7 0.7 %select_rows.1 = (bf16[1,2,256,512]{3,2,1,0:T(8,128)(2,1)S(1)}, bf16[1,2,256,512]{3,2,1,0:T(8,128)(2,1)S(1)}) custom-call(s32[1,2]{1,0:T(1,128)S(1)} %copy-done.3, f32[32,128]{1,0:T(8,128)} %sum_squares.1.order_ref, bf16[2,256,512]{2,1,0:T(8,128)(2,1)S(1)} %copy-done.2, bf16[2,256,512]{2,1,0:T(8,128)(2,1)S(1)} %copy-done.1), custom_call_target="tpu_custom_call" | custom-call | bytes 2097152 | tf_op jit(solution)/shard_map/select_rows/pallas_call | solution.py:85
  11.4 0.3 collective-permute-start
  11.7 5.0 %all-to-all-done = f32[32,1,128]{2,1,0:T(1,128)S(1)} async-done(((f32[32,1,128]{2,1,0:T(1,128)}), f32[32,1,128]{2,1,0:T(1,128)S(1)}, u32[]{:S(2)}, u32[]{:S(2)}) %all-to-all-start) | async-done | bytes 16416 | tf_op jit(solution)/shard_map/all_to_all | solution.py:408
  16.7 0.1 clip_factor.1.clip_ref
  16.9 0.0 collective-permute-done.got_ref
  16.9 0.5 %packed_grams.1 = (bf16[1,528,128]{2,1,0:T(8,128)(2,1)S(1)}, bf16[1,528,128]{2,1,0:T(8,128)(2,1)S(1)}, bf16[1,2,256,512]{3,2,1,0:T(8,128)(2,1)S(1)}) custom-call(f32[8,128]{1,0:T(8,128)S(1)} %clip_factor.1.clip_ref, bf16[1,2,256,512]{3,2,1,0:T(8,128)(2,1)S(1)} %get-tuple-element.11.mine_ref, bf16[1,2,256,512]{3,2,1,0:T(8,128)(2,1)S(1)} %collective-permute-done.got_ref), custom_call_target="tpu_custom_call" | custom-call | flops 268435456 | bytes 2097152 | tf_op jit(solution)/shard_map/packed_grams/pallas_call | solution.py:172
  17.4 0.6 %collective-permute-start.1 = (bf16[1,528,128]{2,1,0:T(8,128)(2,1)S(1)}, bf16[1,528,128]{2,1,0:T(8,128)(2,1)S(1)}, u32[]{:S(2)}, u32[]{:S(2)}) collective-permute-start(bf16[1,528,128]{2,1,0:T(8,128)(2,1)S(1)} %get-tuple-element.13), channel_id=1, source_target_pairs={{0,8},{4,12},{8,0},{12,4},{16,24},{20,28},{24,16},{28,20},{1,9},{5... | collective-permute-start | bytes 405512 | tf_op jit(solution)/shard_map/ppermute | solution.py:405
  18.0 0.5 %collective-permute-start.3 = (bf16[1,528,128]{2,1,0:T(8,128)(2,1)S(1)}, bf16[1,528,128]{2,1,0:T(8,128)(2,1)S(1)}, u32[]{:S(2)}, u32[]{:S(2)}) collective-permute-start(bf16[1,528,128]{2,1,0:T(8,128)(2,1)S(1)} %get-tuple-element.17), channel_id=1, source_target_pairs={{0,16},{4,20},{8,24},{12,28},{16,0},{20,4},{24,8},{28,12},{1,17},{... | collective-permute-start | bytes 405512 | tf_op jit(solution)/shard_map/ppermute | solution.py:405
  18.5 0.9 %update_momentum.1 = bf16[2,256,512]{2,1,0:T(8,128)(2,1)} custom-call(f32[8,128]{1,0:T(8,128)S(1)} %clip_factor.1.clip_ref, bf16[1,2,256,512]{3,2,1,0:T(8,128)(2,1)S(1)} %get-tuple-element.14.rows_ref, bf16[1,2,256,512]{3,2,1,0:T(8,128)(2,1)S(1)} %get-tuple-element.12.theirs_ref), custom_call_target="tpu_custom_call" | custom-call | flops 786432 | bytes 1572864 | tf_op jit(solution)/shard_map/update_momentum/pallas_call | solution.py:210
  19.4 3.2 %collective-permute-done.1 = bf16[1,528,128]{2,1,0:T(8,128)(2,1)S(1)} collective-permute-done((bf16[1,528,128]{2,1,0:T(8,128)(2,1)S(1)}, bf16[1,528,128]{2,1,0:T(8,128)(2,1)S(1)}, u32[]{:S(2)}, u32[]{:S(2)}) %collective-permute-start.1) | collective-permute-done | bytes 135200 | tf_op jit(solution)/shard_map/ppermute | solution.py:405
  22.7 0.7 %collective-permute-start.2 = (bf16[1,528,128]{2,1,0:T(8,128)(2,1)S(1)}, bf16[1,528,128]{2,1,0:T(8,128)(2,1)S(1)}, u32[]{:S(2)}, u32[]{:S(2)}) collective-permute-start(bf16[1,528,128]{2,1,0:T(8,128)(2,1)S(1)} %add_convert_fusion.1.a0_ref), channel_id=1, source_target_pairs={{0,16},{4,20},{8,24},{12,28},{16,0},{20,4},{24,8},{28,12},{1,17},{... | collective-permute-start | bytes 405512 | tf_op jit(solution)/shard_map/ppermute | solution.py:405
  23.4 0.0 collective-permute-done.3
  23.4 1.1 %collective-permute-start.4 = (bf16[1,528,128]{2,1,0:T(8,128)(2,1)S(1)}, bf16[1,528,128]{2,1,0:T(8,128)(2,1)S(1)}, u32[]{:S(2)}, u32[]{:S(2)}) collective-permute-start(bf16[1,528,128]{2,1,0:T(8,128)(2,1)S(1)} %add_convert_fusion.b0_ref), channel_id=1, source_target_pairs={{0,8},{4,12},{8,0},{12,4},{16,24},{20,28},{24,16},{28,20},{1,9},{5... | collective-permute-start | bytes 405512 | tf_op jit(solution)/shard_map/ppermute | solution.py:405
  24.6 3.2 %collective-permute-done.2.a1_ref = bf16[1,528,128]{2,1,0:T(8,128)(2,1)S(1)} collective-permute-done((bf16[1,528,128]{2,1,0:T(8,128)(2,1)S(1)}, bf16[1,528,128]{2,1,0:T(8,128)(2,1)S(1)}, u32[]{:S(2)}, u32[]{:S(2)}) %collective-permute-start.2) | collective-permute-done | bytes 135200 | tf_op jit(solution)/shard_map/ppermute | solution.py:405
  27.8 0.7 %collective-permute-done.4.b1_ref = bf16[1,528,128]{2,1,0:T(8,128)(2,1)S(1)} collective-permute-done((bf16[1,528,128]{2,1,0:T(8,128)(2,1)S(1)}, bf16[1,528,128]{2,1,0:T(8,128)(2,1)S(1)}, u32[]{:S(2)}, u32[]{:S(2)}) %collective-permute-start.4) | collective-permute-done | bytes 135200 | tf_op jit(solution)/shard_map/ppermute | solution.py:405
  28.5 1.9 %newton_factors.1 = (bf16[1,512,512]{2,1,0:T(8,128)(2,1)S(1)}, bf16[1,256,512]{2,1,0:T(8,128)(2,1)S(1)}) custom-call(bf16[1,528,128]{2,1,0:T(8,128)(2,1)S(1)} %add_convert_fusion.1.a0_ref, bf16[1,528,128]{2,1,0:T(8,128)(2,1)S(1)} %collective-permute-done.2.a1_ref, bf16[1,528,128]{2,1,0:T(8,128)(2,1)S(1)} %add_convert_fusion.b0_ref, ...), custom_call_target="tpu_custom_call" | custom-call | flops 1342177280 | bytes 1064960 | tf_op jit(solution)/shard_map/newton_factors/pallas_call | solution.py:317
  30.4 0.1 collective-permute-start.5
  30.5 1.0 %update_own.1.update_ref = bf16[2,256,512]{2,1,0:T(8,128)(2,1)} custom-call(bf16[1,2,256,512]{3,2,1,0:T(8,128)(2,1)S(1)} %get-tuple-element.14.rows_ref, bf16[1,512,512]{2,1,0:T(8,128)(2,1)S(1)} %get-tuple-element.19.factor_ref), custom_call_target="tpu_custom_call" | custom-call | flops 134217728 | bytes 786432 | tf_op jit(solution)/shard_map/update_own/pallas_call | solution.py:357
  31.5 0.5 %collective-permute-done.5.got_ref = bf16[1,256,512]{2,1,0:T(8,128)(2,1)S(1)} collective-permute-done((bf16[1,256,512]{2,1,0:T(8,128)(2,1)S(1)}, bf16[1,256,512]{2,1,0:T(8,128)(2,1)S(1)}, u32[]{:S(2)}, u32[]{:S(2)}) %collective-permute-start.5) | collective-permute-done | bytes 262176 | tf_op jit(solution)/shard_map/ppermute | solution.py:405
  32.0 0.7 %update_other.1 = bf16[2,256,512]{2,1,0:T(8,128)(2,1)} custom-call(bf16[1,256,512]{2,1,0:T(8,128)(2,1)S(1)} %collective-permute-done.5.got_ref, bf16[2,256,512]{2,1,0:T(8,128)(2,1)} %update_own.1.update_ref), custom_call_target="tpu_custom_call", output_to_operand_aliasing={{}: (1, {})} | custom-call | bytes 524288 | tf_op jit(solution)/shard_map/update_other/pallas_call | solution.py:381
  (2 shorter events, 0.1 us)
Async XLA Ops:
  0.6 1.0 %copy-start = (bf16[2,256,512]{2,1,0:T(8,128)(2,1)S(1)}, bf16[2,256,512]{2,1,0:T(8,128)(2,1)}, u32[]{:S(2)}) copy-start(bf16[2,256,512]{2,1,0:T(8,128)(2,1)} %grads_ref.1) | copy-start | bytes 1572868
  1.7 8.0 %copy-start.1 = (bf16[2,256,512]{2,1,0:T(8,128)(2,1)S(1)}, bf16[2,256,512]{2,1,0:T(8,128)(2,1)}, u32[]{:S(2)}) copy-start(bf16[2,256,512]{2,1,0:T(8,128)(2,1)} %grads_ref.1) | copy-start | bytes 1572868
  2.3 7.3 %copy-start.3 = (s32[1,2]{1,0:T(1,128)S(1)}, s32[1,2]{1,0:T(1,128)}, u32[]{:S(2)}) copy-start(s32[1,2]{1,0:T(1,128)} %slot_ref.1) | copy-start | bytes 28
  2.3 14.4 %all-to-all-start = ((f32[32,1,128]{2,1,0:T(1,128)}), f32[32,1,128]{2,1,0:T(1,128)S(1)}, u32[]{:S(2)}, u32[]{:S(2)}) async-start(f32[32,1,128]{2,1,0:T(1,128)} %bitcast.2), calls=%async_computation | async-start | bytes 32768 | tf_op jit(solution)/shard_map/all_to_all | solution.py:408
  9.7 1.0 %copy-start.2 = (bf16[2,256,512]{2,1,0:T(8,128)(2,1)S(1)}, bf16[2,256,512]{2,1,0:T(8,128)(2,1)}, u32[]{:S(2)}) copy-start(bf16[2,256,512]{2,1,0:T(8,128)(2,1)} %momentum_ref.1) | copy-start | bytes 1572868
  11.4 5.5 %collective-permute-start = (bf16[1,2,256,512]{3,2,1,0:T(8,128)(2,1)S(1)}, bf16[1,2,256,512]{3,2,1,0:T(8,128)(2,1)S(1)}, u32[]{:S(2)}, u32[]{:S(2)}) collective-permute-start(bf16[1,2,256,512]{3,2,1,0:T(8,128)(2,1)S(1)} %get-tuple-element.12.theirs_ref), channel_id=1, source_target_pairs={{0,4},{4,0},{8,12},{12,8},{16,20},{20,16},{24,28},{28,24},{1,5},{5... | collective-permute-start | bytes 1572872 | tf_op jit(solution)/shard_map/ppermute | solution.py:405
  17.4 5.3 %collective-permute-start.1 = (bf16[1,528,128]{2,1,0:T(8,128)(2,1)S(1)}, bf16[1,528,128]{2,1,0:T(8,128)(2,1)S(1)}, u32[]{:S(2)}, u32[]{:S(2)}) collective-permute-start(bf16[1,528,128]{2,1,0:T(8,128)(2,1)S(1)} %get-tuple-element.13), channel_id=1, source_target_pairs={{0,8},{4,12},{8,0},{12,4},{16,24},{20,28},{24,16},{28,20},{1,9},{5... | collective-permute-start | bytes 405512 | tf_op jit(solution)/shard_map/ppermute | solution.py:405
  18.0 5.4 %collective-permute-start.3 = (bf16[1,528,128]{2,1,0:T(8,128)(2,1)S(1)}, bf16[1,528,128]{2,1,0:T(8,128)(2,1)S(1)}, u32[]{:S(2)}, u32[]{:S(2)}) collective-permute-start(bf16[1,528,128]{2,1,0:T(8,128)(2,1)S(1)} %get-tuple-element.17), channel_id=1, source_target_pairs={{0,16},{4,20},{8,24},{12,28},{16,0},{20,4},{24,8},{28,12},{1,17},{... | collective-permute-start | bytes 405512 | tf_op jit(solution)/shard_map/ppermute | solution.py:405
  22.7 5.1 %collective-permute-start.2 = (bf16[1,528,128]{2,1,0:T(8,128)(2,1)S(1)}, bf16[1,528,128]{2,1,0:T(8,128)(2,1)S(1)}, u32[]{:S(2)}, u32[]{:S(2)}) collective-permute-start(bf16[1,528,128]{2,1,0:T(8,128)(2,1)S(1)} %add_convert_fusion.1.a0_ref), channel_id=1, source_target_pairs={{0,16},{4,20},{8,24},{12,28},{16,0},{20,4},{24,8},{28,12},{1,17},{... | collective-permute-start | bytes 405512 | tf_op jit(solution)/shard_map/ppermute | solution.py:405
  23.4 5.1 %collective-permute-start.4 = (bf16[1,528,128]{2,1,0:T(8,128)(2,1)S(1)}, bf16[1,528,128]{2,1,0:T(8,128)(2,1)S(1)}, u32[]{:S(2)}, u32[]{:S(2)}) collective-permute-start(bf16[1,528,128]{2,1,0:T(8,128)(2,1)S(1)} %add_convert_fusion.b0_ref), channel_id=1, source_target_pairs={{0,8},{4,12},{8,0},{12,4},{16,24},{20,28},{24,16},{28,20},{1,9},{5... | collective-permute-start | bytes 405512 | tf_op jit(solution)/shard_map/ppermute | solution.py:405
  30.4 1.6 %collective-permute-start.5 = (bf16[1,256,512]{2,1,0:T(8,128)(2,1)S(1)}, bf16[1,256,512]{2,1,0:T(8,128)(2,1)S(1)}, u32[]{:S(2)}, u32[]{:S(2)}) collective-permute-start(bf16[1,256,512]{2,1,0:T(8,128)(2,1)S(1)} %get-tuple-element.18), channel_id=1, source_target_pairs={{0,4},{4,0},{8,12},{12,8},{16,20},{20,16},{24,28},{28,24},{1,5},{5... | collective-permute-start | bytes 786440 | tf_op jit(solution)/shard_map/ppermute | solution.py:405
